TPU v7x, 32 devices: a whole 2x2x4 slice. The times are simulated.
32 devices in a mesh: dp: 8 (over z, y), seq: 4 (over x, core).
Axes of the slice: x: 2, y: 2, z: 4, core: 2. Of those that a mesh axis runs over, the one named last changes fastest.
Arguments:
- frames: bfloat16 [8, 1536, 1024], P('dp', 'seq'), may hold values from -6 to 6
- output_gradient: bfloat16 [8, 1536, 1024], P('dp', 'seq'), may hold values from -6 to 6
- segment_lengths: int32 [8, 4], P('dp'), may hold values from 1 to 1533, as said below
- time_index: int32 [8, 4], P('dp'), may hold values from 0 to 999
- query_weight: bfloat16 [1024, 1024], P(('dp', 'seq')), may hold values from -0.1875 to 0.1875
- query_bias: bfloat16 [1024], P(('dp', 'seq')), may hold values from -3 to 3
- key_weight: bfloat16 [1024, 1024], P(('dp', 'seq')), may hold values from -0.1875 to 0.1875
- key_bias: bfloat16 [1024], P(('dp', 'seq')), may hold values from -3 to 3
- value_weight: bfloat16 [1024, 1024], P(('dp', 'seq')), may hold values from -0.1875 to 0.1875
- value_bias: bfloat16 [1024], P(('dp', 'seq')), may hold values from -3 to 3
- output_projection: bfloat16 [1024, 1024], P(('dp', 'seq')), may hold values from -2.5 to 2.5
- output_bias: bfloat16 [1024], P(('dp', 'seq')), may hold values from -3 to 3
- up_weight: bfloat16 [1024, 2048], P(('dp', 'seq')), may hold values from -0.1875 to 0.1875
- up_bias: bfloat16 [2048], P(('dp', 'seq')), may hold values from -3 to 3
- down_weight: bfloat16 [2048, 1024], P(('dp', 'seq')), may hold values from -0.125 to 0.125
- down_bias: bfloat16 [1024], P(('dp', 'seq')), may hold values from -3 to 3
- modulation_weight: bfloat16 [1024, 6144], P(('dp', 'seq')), may hold values from -0.1875 to 0.1875
- modulation_bias: bfloat16 [6144], P(('dp', 'seq')), may hold values from -3 to 3
Outputs:
- layer_output: bfloat16 [8, 1536, 1024], P('dp', 'seq')
- frames_grad: bfloat16 [8, 1536, 1024], P('dp', 'seq')
- query_weight_grad: float32 [1024, 1024], P(('dp', 'seq'))
- query_bias_grad: float32 [1024], P(('dp', 'seq'))
- key_weight_grad: float32 [1024, 1024], P(('dp', 'seq'))
- key_bias_grad: float32 [1024], P(('dp', 'seq'))
- value_weight_grad: float32 [1024, 1024], P(('dp', 'seq'))
- value_bias_grad: float32 [1024], P(('dp', 'seq'))
- output_weight_grad: float32 [1024, 1024], P(('dp', 'seq'))
- output_bias_grad: float32 [1024], P(('dp', 'seq'))
- up_weight_grad: float32 [1024, 2048], P(('dp', 'seq'))
- up_bias_grad: float32 [2048], P(('dp', 'seq'))
- down_weight_grad: float32 [2048, 1024], P(('dp', 'seq'))
- down_bias_grad: float32 [1024], P(('dp', 'seq'))
- modulation_weight_grad: float32 [1024, 6144], P(('dp', 'seq'))
- modulation_bias_grad: float32 [6144], P(('dp', 'seq'))
Inputs may be any that keep to these rules, and one draw needn't show every extreme that they name: `segment_lengths`: in each packed row the 4 lengths sum to 1536; one utterance is longer than 1152, the others shorter than 96; in one row of every draw the others have a single frame each.
All inputs are finite; a program needn't handle non-finite values.
Results may differ from a plain program's by a relative error of at most 0.035.
Values may be sent and summed in bfloat16 or wider, within the bound.
A program may use at most 192 MiB of HBM per device.

v0:
```python
from functools import partial
import math

import jax
import jax.numpy as jnp
from jax import lax
from jax.experimental import pallas as pl
from jax.experimental.pallas import tpu as pltpu
from jax.sharding import PartitionSpec as P

HEAD_DIM = 64
MODEL_WIDTH = 1024
SEGS = 4
EPSILON = 1e-06
NEGATIVE = -1e30
HIGHEST = lax.Precision.HIGHEST
F32 = jnp.float32
BF16 = jnp.bfloat16
LANES = 128


class Mover:
    def __init__(self, send_sems, recv_sems, local_sems):
        self.send_sems, self.recv_sems, self.local_sems = send_sems, recv_sems, local_sems
        self.count = self.local_count = 0
        self.sent = []

    def send(self, source, target, device):
        slot = self.count
        self.count += 1
        copy = pltpu.make_async_remote_copy(
            src_ref=source,
            dst_ref=target,
            send_sem=self.send_sems.at[slot],
            recv_sem=self.recv_sems.at[slot],
            device_id=device,
            device_id_type=pl.DeviceIdType.MESH,
        )
        copy.start()
        self.sent.append(copy)
        return copy

    def local(self, source, target):
        slot = self.local_count
        self.local_count += 1
        copy = pltpu.make_async_copy(source, target, self.local_sems.at[slot])
        copy.start()
        return copy

    def finish(self, but=()):
        for copy in self.sent:
            if not any(copy is other for other in but):
                copy.wait_send()


class Place:
    def __init__(self, depth):
        dp, seq = lax.axis_index("dp"), lax.axis_index("seq")
        self.depth = depth
        self.z, self.y = dp // 2, dp % 2
        self.x, self.c = seq // 2, seq % 2
        self.seq = seq
        self.index = dp * 4 + seq

    def at(self, z, y, x, c):
        return {"dp": z * 2 + y, "seq": x * 2 + c}

    def core(self):
        return self.at(self.z, self.y, self.x, 1 - self.c)

    def across_x(self):
        return self.at(self.z, self.y, 1 - self.x, self.c)

    def across_y(self):
        return self.at(self.z, 1 - self.y, self.x, self.c)

    def ahead(self, step):
        return (self.z + step) % self.depth

    def along_z(self, step):
        return self.at(self.ahead(step), self.y, self.x, self.c)

    def row_peer(self, step):
        return {"dp": self.z * 2 + self.y, "seq": (self.seq + step) % 4}

    def enter(self, diagonal=False):
        barrier = pltpu.get_barrier_semaphore()
        peers = [self.row_peer(step) for step in (1, 2, 3)] + [self.across_y()]
        peers += [self.along_z(step) for step in range(1, self.depth)]
        if diagonal:
            peers += [self.at(self.ahead(k), 1 - self.y, self.x, self.c) for k in range(1, self.depth)]
        for peer in peers:
            pl.semaphore_signal(barrier, 1, device_id=peer, device_id_type=pl.DeviceIdType.MESH)
        pl.semaphore_wait(barrier, len(peers))


def lanes_of(shape, axis=1):
    return lax.broadcasted_iota(jnp.int32, shape, axis)


def frame_segments(lens, first_row, rows, width):
    position = lanes_of((rows, width), 0) + first_row
    first, second, third = lens[0, 0], lens[0, 0] + lens[0, 1], lens[0, 0] + lens[0, 1] + lens[0, 2]
    segment = (
        (position >= first).astype(jnp.int32)
        + (position >= second).astype(jnp.int32)
        + (position >= third).astype(jnp.int32)
    )
    start = jnp.where(
        segment == 0, 0, jnp.where(segment == 1, first, jnp.where(segment == 2, second, third))
    )
    return segment, position - start


def three_parts(values):
    high = values.astype(BF16).astype(F32)
    rest = values - high
    middle = rest.astype(BF16).astype(F32)
    return high, middle, (rest - middle).astype(BF16).astype(F32)


def swap_halves(values, lane):
    return jnp.where(
        lane % HEAD_DIM < HEAD_DIM // 2, pltpu.roll(values, 96, 1), pltpu.roll(values, 32, 1)
    )


def head_only(values, lane, head):
    return jnp.where((lane >= HEAD_DIM) == bool(head), values.astype(F32), 0.0).astype(BF16)


def across(left, right):
    return lax.dot_general(left, right, (((1,), (1,)), ((), ())), preferred_element_type=F32)


def product(left, right):
    return jnp.dot(left, right, preferred_element_type=F32)


AXES = (
    (1, 2, 0), (0, 2, 1), (2, 0, 1), (0, 2, 1), (0, 1, 2), (0, 1, 2), (0, 2, 1), (0, 2, 1), (2, 1, 0), (0, 1, 2),
)
(
    GATHER_Z, GATHER_TWO, GATHER_THREE, GATHER_CORE, COLUMNS_Z, COLUMNS_Y, PROJECT, ATTEND, GO_UP, FRAMES_X,
    FRAMES_ON, TABLES, TIMES_Y, SHARE, MOD_Y, MOD_Z, MOD_X, MOD_LAST, FRAMES_CORE, BIAS_Y, BIAS_X, BIAS_CORE,
    BIASES, MODS, OUT, GO_DOWN, BACK, GRADS, WAITS,
) = range(29)
FORWARD_ORDER = (
    (FRAMES_X, 0), (GATHER_Z, 9), (GATHER_Z, 1), (TIMES_Y, 0), (BIAS_Y, 0), (FRAMES_CORE, 0), (GATHER_TWO, 9),
    (COLUMNS_Z, 0), (COLUMNS_Z, 1), (SHARE, 0), (GATHER_Z, 4), (GATHER_Z, 8), (BIAS_X, 0), (MOD_Y, 0),
    (COLUMNS_Y, 0), (GATHER_THREE, 9), (COLUMNS_Y, 1), (COLUMNS_Z, 2), (FRAMES_X, 1), (GATHER_Z, 3), (MOD_Z, 0),
    (GATHER_Z, 0), (GATHER_Z, 2), (GATHER_Z, 7), (GATHER_TWO, 8), (GATHER_Z, 6), (TABLES, 1), (BIAS_CORE, 0),
    (GATHER_TWO, 4), (BIASES, 0), (COLUMNS_Y, 2), (TABLES, 0), (GATHER_TWO, 0), (GATHER_TWO, 1), (FRAMES_ON, 1),
    (MOD_X, 0), (GATHER_Z, 5), (GATHER_TWO, 3), (GATHER_THREE, 1), (GATHER_TWO, 2), (MOD_LAST, 0),
    (GATHER_THREE, 4), (MODS, 0), (PROJECT, 0), (GATHER_CORE, 9), (GATHER_THREE, 3), (GATHER_TWO, 7),
    (FRAMES_ON, 0), (PROJECT, 1), (PROJECT, 2), (GATHER_THREE, 0), (GATHER_TWO, 6), (PROJECT, 3),
    (GATHER_CORE, 1), (GATHER_TWO, 5), (GATHER_THREE, 8), (ATTEND, 1), (GATHER_THREE, 2), (ATTEND, 1),
    (GATHER_CORE, 4), (GATHER_CORE, 3), (GATHER_THREE, 5), (GATHER_THREE, 6), (ATTEND, 2), (GATHER_THREE, 7),
    (ATTEND, 3), (GATHER_CORE, 0), (ATTEND, 1), (GATHER_CORE, 6), (GATHER_CORE, 2), (GATHER_CORE, 5), (OUT, 0),
    (GO_UP, 0), (GATHER_CORE, 7), (GATHER_CORE, 8), (GO_UP, 1), (GO_DOWN, 0), (BACK, 0), (GRADS, 0),
)


def forward_kernel(
    depth,
    lens, times, frames, given_in, bq, bk, bv, bo, bu, bd, bm, wq, wk, wv, wo, up, down, mw,
    output, gmid, mg, btile, mods, low, gwo, gup, gdown, do_all, qs_out, ks_out, vs_out, oh_out, lse_out,
    normed_out, wg_out, cos_out, sin_out,
    att, oh, qs, lse, normed, wg, cosr, sinr, rowbias, wo_all, up_all, down_all,
    bb, xall, mwst, tb, part, recva, suma, recvb, sumb, recvc, sumc, recvd, modh, bmat, mod3, qbias,
    ka, va, qaug, given, mod6, branch, middle, normed_two, active, slope, gbt, gh, gn, gb, ga, sums,
    send_sems, recv_sems, local_sems,
):
    here = Place(depth)
    z, y, x, c, g = here.z, here.y, here.x, here.c, here.seq
    span, width = frames.shape
    hidden = up.shape[1]
    rows_all = span * 4
    block, tall, tile = 128, span, 256
    move = Mover(send_sems, recv_sems, local_sems)
    steps_z = range(1, depth)

    row = lanes_of((16, LANES), 0) % 4
    own_times = jnp.where(
        row == 0, times[0, 0], jnp.where(row == 1, times[0, 1], jnp.where(row == 2, times[0, 2], times[0, 3]))
    )
    tb[z, y] = own_times.astype(F32)
    bb[z, y, x, c] = jnp.zeros((8, LANES), F32)
    for n, vector in enumerate((bq, bk, bv, bo, bu, bd)):
        bb[z, y, x, c, n : n + 1, : vector.shape[1]] = vector[...].astype(F32)
    bb[z, y, x, c, 6:7, :] = bm[:, :LANES].astype(F32)
    bb[z, y, x, c, 7:8, : bm.shape[1] - LANES] = bm[:, LANES:].astype(F32)
    weights = (wq, wk, wv)
    own_width = wg.shape[-1]
    locals_first = [
        move.local(weights[j].at[:, pl.ds(pl.multiple_of(g * own_width, LANES), own_width)], wg.at[j, z, y, g])
        for j in range(3)
    ]
    strip = mw.shape[1] // 4
    local_mw = [
        move.local(mw.at[:, pl.ds(j * strip, strip)], mwst.at[pl.ds(j * 32, 32)]) for j in range(4)
    ]
    local_frames = move.local(frames, xall.at[g])
    local_given = move.local(given_in, given)
    here.enter()

    legs = {}
    shard, wide = wo.shape[0], MODEL_WIDTH
    thin = shard // 2
    flows = []

    def add_flow(source, target, first_row, columns=None):
        rows = pl.ds(first_row, thin)
        if columns is None:
            flows.append((source.at[rows], target.at[:, :, :, :, rows]))
        else:
            columns = pl.ds(columns, wide)
            flows.append((source.at[rows, columns], target.at[:, :, :, :, rows, columns]))

    for side in range(2):
        add_flow(wo, wo_all, side * thin)
    for side in range(2):
        add_flow(up, up_all, side * thin, 0)
        add_flow(up, up_all, side * thin, wide)
    for side in range(4):
        add_flow(down, down_all, side * thin)
    count = len(flows)

    legs, outgoing, owned = {}, [], {}
    here_at = (z, y, x)

    def to_axis(axis):
        if axis == 0:
            return [here.along_z(k) for k in steps_z]
        return [here.across_y() if axis == 1 else here.across_x()]

    def held(number, known):
        place = tuple(slice(None) if axis in known else here_at[axis] for axis in range(3))
        return flows[number][1].at[place + (c,)]

    def first_leg(number):
        source = flows[number][0]
        target = held(number, ())
        owned[number] = move.local(source, target)
        legs[number] = [move.send(source, target, peer) for peer in to_axis(AXES[number][0])]

    def next_leg(number, done):
        if done == 1:
            owned[number].wait()
        for copy in legs[number]:
            copy.wait_recv()
        part = held(number, AXES[number][:done])
        peers = [here.core()] if done == 3 else to_axis(AXES[number][done])
        legs[number] = [move.send(part, part, peer) for peer in peers]
        outgoing.extend(legs[number])

    def second_leg(number):
        next_leg(number, 1)

    def third_leg(number):
        next_leg(number, 2)

    def fourth_leg(number):
        next_leg(number, 3)

    def arrived(*numbers):
        for number in numbers:
            for copy in legs[number]:
                copy.wait_recv()

    times_z = [move.send(tb.at[z, y], tb.at[z, y], here.along_z(k)) for k in steps_z]
    qkv_row = [
        [
            move.send(
                weights[j].at[:, pl.ds(pl.multiple_of((g + k) % 4 * own_width, LANES), own_width)],
                wg.at[j, z, y, g],
                here.row_peer(k),
            )
            for k in (1, 2, 3)
        ]
        for j in range(3)
    ]
    bias_z = [move.send(bb.at[z, y, x, c], bb.at[z, y, x, c], here.along_z(k)) for k in steps_z]
    part_rows = span // 2
    frame_parts = [pl.ds(n * part_rows, part_rows) for n in range(2)]
    half = strip // 2
    sent = {}
    stores = []

    def columns_z(j):
        locals_first[j].wait()
        for copy in qkv_row[j]:
            copy.wait_recv()
        sent["q", j] = [move.send(wg.at[j, z, y], wg.at[j, z, y], here.along_z(k)) for k in steps_z]

    def columns_y(j):
        for copy in sent["q", j]:
            copy.wait_recv()
        sent["p", j] = move.send(wg.at[j, :, y], wg.at[j, :, y], here.across_y())

    def times_across():
        for copy in times_z:
            copy.wait_recv()
        sent["ty"] = move.send(tb.at[:, y], tb.at[:, y], here.across_y())

    def mod_share():
        sent["ty"].wait_recv()
        lane = lanes_of((16 * 2 * depth, LANES))
        row = lanes_of((16 * 2 * depth, LANES), 0)
        feature = here.index * 32 + lane % 32
        halfway = MODEL_WIDTH // 2
        frequency = jnp.exp((feature % halfway).astype(F32) * (-math.log(10000.0) / halfway))
        angle = tb[...].reshape(16 * 2 * depth, LANES) * frequency
        wave = jnp.where(feature < halfway, jnp.sin(angle), jnp.cos(angle))
        gated = wave / (1.0 + jnp.exp(-wave))
        low[...] = jnp.where(lane // 32 == (row % 16) // 4, gated, 0.0).astype(BF16)
        for copy in local_mw:
            copy.wait()
        for side in range(2):
            share = product(low[...], mwst[:, side * half : (side + 1) * half])
            part[side] = share.astype(BF16).reshape(depth, 2, 16, half)
        sent["mc"] = move.send(part.at[1 - c], recva, here.core())

    def mod_y():
        sent["mc"].wait_recv()
        suma[...] = (part[c].astype(F32) + recva[...].astype(F32)).astype(BF16)
        sent["my"] = move.send(suma.at[:, 1 - y], recvb, here.across_y())

    def mod_z():
        sent["my"].wait_recv()
        sumb[...] = (suma[:, y].astype(F32) + recvb[...].astype(F32)).astype(BF16)
        sent["mz"] = [move.send(sumb.at[here.ahead(k)], recvc.at[k - 1], here.along_z(k)) for k in steps_z]

    def mod_x():
        total = sumb[z].astype(F32)
        for k in steps_z:
            sent["mz"][k - 1].wait_recv()
            total = total + recvc[k - 1].astype(F32)
        sumc[...] = total
        sent["mx"] = move.send(sumc, recvd, here.across_x())

    def mod_last():
        sent["mx"].wait_recv()
        modh[c] = sumc[...] + recvd[...]
        sent["ml"] = move.send(modh.at[c], modh.at[c], here.core())

    def frames_core():
        sent["fc"] = move.send(frames, xall.at[g], here.core())

    def frames_x(n):
        sent["fx", n] = move.send(frames.at[frame_parts[n]], xall.at[g, frame_parts[n]], here.across_x())

    frames_here = []

    def frames_in(n):
        if n not in frames_here:
            sent["fx", n].wait_recv()
            frames_here.append(n)

    def frames_on(n):
        frames_in(n)
        theirs = xall.at[(g + 2) % 4, frame_parts[n]]
        sent["on", n] = move.send(theirs, theirs, here.core())

    def bias_y():
        for copy in bias_z:
            copy.wait_recv()
        sent["by"] = move.send(bb.at[:, y, x, c], bb.at[:, y, x, c], here.across_y())

    def bias_x():
        sent["by"].wait_recv()
        sent["bx"] = move.send(bb.at[:, :, x, c], bb.at[:, :, x, c], here.across_x())

    def bias_core():
        sent["bx"].wait_recv()
        sent["bc"] = move.send(bb.at[:, :, :, c], bb.at[:, :, :, c], here.core())

    def tables(step, carry):
        rows = pl.ds(pl.multiple_of(step * block, block), block)
        segment, relative = frame_segments(lens, step * block, block, LANES)
        lane = lanes_of((block, LANES))
        quarter = HEAD_DIM // 2
        frequency = jnp.exp((lane % quarter).astype(F32) * (-math.log(10000.0) / quarter))
        angle = relative.astype(F32) * frequency
        cosr[rows, :] = jnp.cos(angle)
        sine = jnp.sin(angle)
        sinr[rows, :] = jnp.where(lane % HEAD_DIM < quarter, -sine, sine)
        same = segment == lane
        qaug[rows, :] = jnp.where((lane < SEGS) & jnp.logical_not(same), NEGATIVE, 0.0).astype(BF16)
        keyside = jnp.where((lane < SEGS) & same, 1.0, jnp.where((lane >= 4) & (lane < 7), 1.0, 0.0))
        for pair in range(2):
            ka[pair, rows, LANES:] = keyside.astype(BF16)
            va[pair, rows, LANES:] = jnp.where(lane < 3, 1.0, 0.0).astype(BF16)
        return carry

    def tables_half(n):
        lax.fori_loop(n * rows_all // (2 * block), (n + 1) * rows_all // (2 * block), tables, 0)

    def bias_vectors():
        sent["bc"].wait_recv()
        bmat[...] = bb[...].reshape(16 * 2 * depth * 2, LANES).astype(BF16)

        place = lanes_of((LANES, own_width), 0)
        column = lanes_of((LANES, own_width))
        brow, bcol = lanes_of((64, own_width), 0), lanes_of((64, own_width))
        spread = jnp.where(column % 32 == place, 1.0, 0.0).astype(BF16)
        for j in range(3):
            mine = (brow % 8 == j) & (brow // 8 == bcol // 32)
            held = product(bmat[pl.ds(pl.multiple_of(g * 64, 64), 64), :], spread)
            qbias[j : j + 1, :] = jnp.sum(jnp.where(mine, held, 0.0), axis=0, keepdims=True)

        trow, tcol = lanes_of((16 * 2 * depth * 2, tile), 0), lanes_of((16 * 2 * depth * 2, tile))
        place, column = lanes_of((LANES, tile), 0), lanes_of((LANES, tile))

        def row_vector(step, size, source):
            spread = jnp.where(column % size == place, 1.0, 0.0).astype(BF16)
            chosen = (trow % 8 == source) & (trow // 8 == (tcol + step * tile) // size)
            return jnp.sum(jnp.where(chosen, product(bmat[...], spread), 0.0), axis=0, keepdims=True)

        def narrow_vectors(step, carry):
            columns = pl.ds(pl.multiple_of(step * tile, tile), tile)
            rowbias[0:1, columns] = row_vector(step, 32, 3)
            rowbias[2:3, columns] = row_vector(step, 32, 5)
            return carry

        def wide_vector(step, carry):
            rowbias[1:2, pl.ds(pl.multiple_of(step * tile, tile), tile)] = row_vector(step, 64, 4)
            return carry

        lax.fori_loop(0, MODEL_WIDTH // tile, narrow_vectors, 0)
        lax.fori_loop(0, up.shape[1] // tile, wide_vector, 0)

        place = lanes_of((LANES, half), 0)
        column = lanes_of((LANES, half))
        spread_a = jnp.where(column % 192 == place, 1.0, 0.0).astype(BF16)
        spread_b = jnp.where(column % 192 == place + LANES, 1.0, 0.0).astype(BF16)
        brow, bcol = lanes_of((32, half), 0), lanes_of((32, half))
        inside = brow // 8 == bcol // 192
        for q in range(8):
            rows = bmat[q * 32 : (q + 1) * 32, :]
            terms = jnp.where(inside & (brow % 8 == 6), product(rows, spread_a), 0.0)
            terms = terms + jnp.where(inside & (brow % 8 == 7), product(rows, spread_b), 0.0)
            mods[4:5, q * half : (q + 1) * half] = jnp.sum(terms, axis=0, keepdims=True)

    def mod_done():
        sent["ml"].wait_recv()
        for q in range(8):
            j, side = q // 2, q % 2
            columns = slice(q * half, (q + 1) * half)
            mods[0:4, columns] = modh[side, 4 * j : 4 * j + 4, :] + mods[4:5, columns]
        for kept, first, last in ((mod3, 0, 2 * width), (mod6, 2 * width, 6 * width)):
            high, mid, rest = three_parts(mods[0:4, first:last])
            kept[0:4, :] = high
            kept[4:8, :] = mid
            kept[8:12, :] = rest
            kept[12:16, :] = jnp.zeros((4, last - first), F32)

    def project_rows(source):
        block, step = span, source
        rows = pl.ds(pl.multiple_of(step * block, block), block)
        values = xall[source].astype(F32)
        center = jnp.mean(values, axis=1, keepdims=True)
        centered = values - center
        variance = jnp.mean(centered * centered, axis=1, keepdims=True)
        segment, _ = frame_segments(lens, step * block, block, 16)
        slot = lanes_of((block, 16))
        chosen = jnp.where((slot < 12) & (slot % 4 == segment), 1.0, 0.0).astype(BF16)
        parts = mod3[...].astype(BF16)
        shift = product(chosen, parts[:, :MODEL_WIDTH])
        scale = product(chosen, parts[:, MODEL_WIDTH:])
        result = (centered * lax.rsqrt(variance + EPSILON) * (1.0 + scale) + shift).astype(BF16)
        normed[rows, :] = result
        cosine, sine = cosr[rows, :], sinr[rows, :]
        lane = lanes_of((block, LANES))
        for j in range(3):
            weight = wg[j].reshape(MODEL_WIDTH, own_width)
            full = product(result, weight) + qbias[j : j + 1, :]
            for pair in range(2):
                piece = full[:, pair * LANES : (pair + 1) * LANES]
                if j < 2:
                    piece = piece * cosine + swap_halves(piece, lane) * sine
                if j == 0:
                    qs[pair, rows, :] = (piece.astype(BF16).astype(F32) * HEAD_DIM**-0.5).astype(BF16)
                elif j == 1:
                    ka[pair, rows, :LANES] = piece.astype(BF16)
                else:
                    va[pair, rows, :LANES] = piece.astype(BF16)

    def project_span(n):
        if n == 0:
            local_frames.wait()
            for j in range(3):
                sent["p", j].wait_recv()
        elif n == 1:
            sent["fc"].wait_recv()
        elif n == 2:
            for m in range(2):
                frames_in(m)
        else:
            for m in range(2):
                sent["on", m].wait_recv()
        number = (g, x * 2 + 1 - c, (1 - x) * 2 + c, (1 - x) * 2 + 1 - c)[n]
        project_rows(number)
        if n == 3:
            for source, target in (
                (qs, qs_out), (ka.at[:, :, pl.ds(0, LANES)], ks_out), (va.at[:, :, pl.ds(0, LANES)], vs_out),
                (normed, normed_out), (wg, wg_out), (cosr, cos_out), (sinr, sin_out),
            ):
                stores.append(move.local(source, target))

    def attend(pair, step):
        rows = pl.ds(pl.multiple_of(step * tall, tall), tall)
        query = qs[pair, rows, :]
        lane = lanes_of((tall, LANES))
        outs, sums = [], []
        for head in range(2):
            left = jnp.concatenate([head_only(query, lane, head), qaug[rows, :]], axis=1)
            scores = across(left, ka[pair])
            highest = jnp.max(scores, axis=1, keepdims=True)
            mixed = product(jnp.exp(scores - highest).astype(BF16), va[pair])
            total = mixed[:, LANES : LANES + 1]
            outs.append(mixed[:, :LANES] / total)
            sums.append(highest + jnp.log(total))
        oh[pair, rows, :] = jnp.where(lane < HEAD_DIM, outs[0], outs[1]).astype(BF16)
        before = jnp.zeros((tall, LANES), F32) if pair == 0 else lse[rows, :]
        lse[rows, :] = jnp.where(
            lane == 2 * pair, sums[0], jnp.where(lane == 2 * pair + 1, sums[1], before)
        )

    delivered = []

    def attend_next():
        pair, at = len(delivered) // 4, len(delivered) % 4
        k = (2, 1, 3, 0)[at]
        target = (g + k) % 4
        attend(pair, target)
        columns = pl.ds(pl.multiple_of(g * own_width + pair * LANES, LANES), LANES)
        source = oh.at[pair, pl.ds(pl.multiple_of(target * span, span), span)]
        if k:
            delivered.append(move.send(source, att.at[:, columns], here.row_peer(k)))
        else:
            delivered.append(move.local(source, att.at[:, columns]))
        if len(delivered) == 8:
            stores.append(move.local(oh, oh_out))
            stores.append(move.local(lse, lse_out))

    base = g * span

    def tile_at(step):
        return pl.ds(pl.multiple_of(step * tile, tile), tile)

    def per_frame(part, first, rows, columns):
        segment, _ = frame_segments(lens, base + first, rows, 16)
        slot = lanes_of((rows, 16))
        chosen = jnp.where((slot < 12) & (slot % 4 == segment), 1.0, 0.0).astype(BF16)
        return product(chosen, mod6[:, columns].astype(BF16))

    def members(first, rows):
        position = base + first + lanes_of((16, rows))
        edges = [lens[0, 0], lens[0, 0] + lens[0, 1], lens[0, 0] + lens[0, 1] + lens[0, 2]]
        inside = sum((position >= edge).astype(jnp.int32) for edge in edges)
        return jnp.where(inside == lanes_of((16, rows), 0), 1.0, 0.0).astype(BF16)

    def by_segment(inside, values):
        top = values.astype(BF16)
        return product(inside, top) + product(inside, (values - top.astype(F32)).astype(BF16))

    def shifted(part, step):
        return pl.ds(pl.multiple_of(part * width + step * tile, tile), tile)

    def wo_columns(columns):
        return wo_all[:, :, :, :, :, columns].reshape(width, tile)

    def up_columns(columns):
        return up_all[:, :, :, :, :, columns].reshape(width, tile)

    def down_columns(columns):
        return down_all[:, :, :, :, :, columns].reshape(hidden, tile)

    def project_out():
        for at, copy in enumerate(delivered):
            copy.wait() if at % 4 == 3 else copy.wait_recv()
        arrived(0, 1)

        def body(step, carry):
            columns = tile_at(step)
            branch[:, columns] = product(att[...], wo_columns(columns)) + rowbias[0:1, columns]
            return carry

        lax.fori_loop(0, width // tile, body, 0)

        def norm_forward(step, carry):
            rows = pl.ds(pl.multiple_of(step * block, block), block)
            gate = per_frame(0, step * block, block, slice(0, width))
            values = xall[g, rows, :].astype(F32) + gate * branch[rows, :]
            middle[rows, :] = values
            centered = values - jnp.mean(values, axis=1, keepdims=True)
            hat = centered * lax.rsqrt(jnp.mean(centered * centered, axis=1, keepdims=True) + EPSILON)
            shift = per_frame(1, step * block, block, slice(width, 2 * width))
            scale = per_frame(2, step * block, block, slice(2 * width, 3 * width))
            normed_two[rows, :] = (hat * (1.0 + scale) + shift).astype(BF16)
            return carry

        lax.fori_loop(0, span // block, norm_forward, 0)

    root = math.sqrt(2.0 / math.pi)

    def go_up(side):
        arrived(2 + side, 4 + side)

        def body(step, carry):
            columns = tile_at(step)
            value = product(normed_two[...], up_columns(columns)) + rowbias[1:2, columns]
            square = value * value
            turn = jnp.tanh(root * value * (1.0 + 0.044715 * square))
            part_one = 0.5 * (1.0 + turn)
            active[:, columns] = (value * part_one).astype(BF16)
            slope[:, columns] = part_one + 0.5 * value * (1.0 - turn * turn) * root * (
                1.0 + 3 * 0.044715 * square
            )
            return carry

        lax.fori_loop(side * width // tile, (side + 1) * width // tile, body, 0)

    def go_down():
        arrived(6, 7, 8, 9)
        local_given.wait()

        def body(step, carry):
            columns = tile_at(step)
            value = product(active[...], down_columns(columns)) + rowbias[2:3, columns]
            gate = per_frame(3, 0, span, shifted(3, step))
            back = given[:, columns].astype(F32)
            output[:, columns] = (middle[:, columns] + gate * value).astype(BF16)
            gbt[:, columns] = (gate * back).astype(BF16)
            sums[:, shifted(3, step)] = by_segment(members(0, span), back * value)
            return carry

        lax.fori_loop(0, width // tile, body, 0)

    def back_values():
        def hidden_tile(step, carry):
            rows = tile_at(step)
            weight = down_all[step // 2, step % 2].reshape(tile, width)
            gh[:, rows] = (across(gbt[...], weight) * slope[:, rows]).astype(BF16)
            return carry

        lax.fori_loop(0, hidden // tile, hidden_tile, 0)

        def normed_tile(step, carry):
            gn[:, tile_at(step)] = across(gh[...], up_all[step].reshape(tile, hidden))
            return carry

        lax.fori_loop(0, width // tile, normed_tile, 0)
        sums[:, : 3 * width] = jnp.zeros((16, 3 * width), F32)

        def norm_back(step, carry):
            rows = pl.ds(pl.multiple_of(step * block, block), block)
            grad, values = gn[rows, :], middle[rows, :]
            centered = values - jnp.mean(values, axis=1, keepdims=True)
            scaled = lax.rsqrt(jnp.mean(centered * centered, axis=1, keepdims=True) + EPSILON)
            hat = centered * scaled
            inner = grad * (1.0 + per_frame(2, step * block, block, slice(2 * width, 3 * width)))
            mean_one = jnp.mean(inner, axis=1, keepdims=True)
            mean_two = jnp.mean(inner * hat, axis=1, keepdims=True)
            total = given[rows, :].astype(F32) + scaled * (inner - mean_one - hat * mean_two)
            gmid[rows, :] = total
            gb[rows, :] = (per_frame(0, step * block, block, slice(0, width)) * total).astype(BF16)
            inside = members(step * block, block)
            sums[:, :width] += by_segment(inside, total * branch[rows, :])
            sums[:, width : 2 * width] += by_segment(inside, grad)
            sums[:, 2 * width : 3 * width] += by_segment(inside, grad * hat)
            return carry

        lax.fori_loop(0, span // block, norm_back, 0)
        sent["o"] = []
        mine = pl.ds(pl.multiple_of(g * span, span), span)
        for k in (1, 2, 3, 0):
            target = (g + k) % 4
            columns = tile_at(target)
            ga[:, columns] = across(gb[...], wo_all[target].reshape(tile, width)).astype(BF16)
            for pair in range(2):
                source = ga.at[:, pl.ds(pl.multiple_of(target * own_width + pair * LANES, LANES), LANES)]
                place = do_all.at[pair, mine]
                if k:
                    sent["o"].append(move.send(source, place, here.row_peer(k)))
                else:
                    stores.append(move.local(source, place))

    def back_weights():
        for copy in outgoing:
            copy.wait_send()

        def down_tile(step, carry):
            grad = from_rows(active[:, tile_at(step)], gbt[...]).astype(BF16)
            down_all[step // 2, step % 2] = grad.reshape(down_all.shape[2:])
            return carry

        lax.fori_loop(0, hidden // tile, down_tile, 0)
        stores.append(move.local(down_all, gdown))

        def up_tile(step, carry):
            grad = from_rows(normed_two[:, tile_at(step)], gh[...]).astype(BF16)
            up_all[step] = grad.reshape(up_all.shape[1:])
            return carry

        lax.fori_loop(0, width // tile, up_tile, 0)
        stores.append(move.local(up_all, gup))

        def out_tile(step, carry):
            grad = from_rows(att[:, tile_at(step)], gb[...]).astype(BF16)
            wo_all[step] = grad.reshape(wo_all.shape[1:])
            return carry

        lax.fori_loop(0, width // tile, out_tile, 0)
        stores.append(move.local(wo_all, gwo))
        ones = jnp.ones((16, span), BF16)
        btile[0:24, :] = jnp.zeros((24, LANES), F32)
        start = 24
        for grads, size in ((gb, width), (gh, hidden), (gbt, width)):
            total = product(ones, grads[...])
            for n in range(size // LANES):
                btile[start + n : start + n + 1, :] = total[0:1, n * LANES : (n + 1) * LANES]
            start += size // LANES
        for n in range(4):
            mg[4 * n : 4 * n + 4, :] = sums[0:4, n * width : (n + 1) * width]

    numbered = {
        GATHER_Z: first_leg, GATHER_TWO: second_leg, GATHER_THREE: third_leg, GATHER_CORE: fourth_leg, COLUMNS_Z: columns_z, COLUMNS_Y: columns_y,
        PROJECT: project_span, GO_UP: go_up, FRAMES_X: frames_x, FRAMES_ON: frames_on, TABLES: tables_half,
    }
    named = {
        TIMES_Y: times_across, SHARE: mod_share, MOD_Y: mod_y, MOD_Z: mod_z, MOD_X: mod_x, MOD_LAST: mod_last,
        FRAMES_CORE: frames_core, BIAS_Y: bias_y, BIAS_X: bias_x, BIAS_CORE: bias_core, BIASES: bias_vectors, MODS: mod_done,
        OUT: project_out, GO_DOWN: go_down, BACK: back_values, GRADS: back_weights,
    }
    for code, number in FORWARD_ORDER:
        if code in named:
            named[code]()
        elif code == ATTEND:
            for _ in range(number):
                attend_next()
        else:
            numbered[code](number)
    for copy in stores:
        copy.wait()
    for copy in sent["o"]:
        copy.wait_recv()
    move.finish(but=outgoing)

def forward_call(depth, span, own_rows, down_rows, hidden, args):
    rows_all, own_width, width = 4 * span, MODEL_WIDTH // 4, MODEL_WIDTH
    half = 6 * MODEL_WIDTH // 8
    vmem, anywhere, scalar = (
        pl.BlockSpec(memory_space=pltpu.VMEM),
        pl.BlockSpec(memory_space=pl.ANY),
        pl.BlockSpec(memory_space=pltpu.SMEM),
    )

    def out(shape, dtype):
        return jax.ShapeDtypeStruct(shape, dtype)

    heads, table = (2, rows_all, LANES), (rows_all, LANES)
    columns = (3, depth, 2, 4, own_rows, own_width)
    wo_shape = (depth, 2, 2, 2, own_rows, width)
    up_shape = (depth, 2, 2, 2, own_rows, hidden)
    down_shape = (depth, 2, 2, 2, down_rows, width)
    outs = [
        (out((span, width), BF16), vmem),
        (out((span, width), F32), vmem),
        (out((16, width), F32), vmem),
        (out((56, LANES), F32), vmem),
        (out((8, 6 * width), F32), vmem),
        (out((32 * depth, LANES), BF16), vmem),
        (out(wo_shape, BF16), anywhere),
        (out(up_shape, BF16), anywhere),
        (out(down_shape, BF16), anywhere),
        (out(heads, BF16), anywhere),
        (out(heads, BF16), anywhere),
        (out(heads, BF16), anywhere),
        (out(heads, BF16), anywhere),
        (out(heads, BF16), anywhere),
        (out(table, F32), anywhere),
        (out((rows_all, width), BF16), anywhere),
        (out(columns, BF16), anywhere),
        (out(table, F32), anywhere),
        (out(table, F32), anywhere),
    ]
    low, wide = pltpu.VMEM((span, width), BF16), pltpu.VMEM((span, width), F32)
    scratch = [
        low,
        pltpu.VMEM(heads, BF16),
        pltpu.VMEM(heads, BF16),
        pltpu.VMEM(table, F32),
        pltpu.VMEM((rows_all, width), BF16),
        pltpu.VMEM(columns, BF16),
        pltpu.VMEM(table, F32),
        pltpu.VMEM(table, F32),
        pltpu.VMEM((8, hidden), F32),
        pltpu.VMEM(wo_shape, BF16),
        pltpu.VMEM(up_shape, BF16),
        pltpu.VMEM(down_shape, BF16),
        pltpu.VMEM((depth, 2, 2, 2, 8, LANES), F32),
        pltpu.VMEM((4, span, width), BF16),
        pltpu.VMEM((LANES, 2 * half), BF16),
        pltpu.VMEM((depth, 2, 16, LANES), F32),
        pltpu.VMEM((2, depth, 2, 16, half), BF16),
        pltpu.VMEM((depth, 2, 16, half), BF16),
        pltpu.VMEM((depth, 2, 16, half), BF16),
        pltpu.VMEM((depth, 16, half), BF16),
        pltpu.VMEM((depth, 16, half), BF16),
        pltpu.VMEM((depth - 1, 16, half), BF16),
        pltpu.VMEM((16, half), F32),
        pltpu.VMEM((16, half), F32),
        pltpu.VMEM((2, 16, half), F32),
        pltpu.VMEM((64 * depth, LANES), BF16),
        pltpu.VMEM((16, 2 * width), F32),
        pltpu.VMEM((8, own_width), F32),
        pltpu.VMEM((2, rows_all, 2 * LANES), BF16),
        pltpu.VMEM((2, rows_all, 2 * LANES), BF16),
        pltpu.VMEM(table, BF16),
        low,
        pltpu.VMEM((16, 4 * width), F32),
        wide,
        wide,
        low,
        pltpu.VMEM((span, hidden), BF16),
        pltpu.VMEM((span, hidden), F32),
        low,
        pltpu.VMEM((span, hidden), BF16),
        wide,
        low,
        low,
        pltpu.VMEM((16, 4 * width), F32),
        pltpu.SemaphoreType.DMA((144,)),
        pltpu.SemaphoreType.DMA((144,)),
        pltpu.SemaphoreType.DMA((48,)),
    ]
    return pl.pallas_call(
        partial(forward_kernel, depth),
        out_shape=[shape for shape, _ in outs],
        in_specs=[scalar, scalar, anywhere, anywhere] + [vmem] * 7 + [anywhere] * 7,
        out_specs=[spec for _, spec in outs],
        scratch_shapes=scratch,
        compiler_params=pltpu.CompilerParams(
            collective_id=0, has_side_effects=True, vmem_limit_bytes=62 * 1024 * 1024
        ),
        cost_estimate=pl.CostEstimate(flops=2 * 10**10, bytes_accessed=60 * 10**6, transcendentals=10**7),
    )(*args)


def turn_back(values, cosine, sine, lane):
    return values * cosine - swap_halves(values, lane) * sine


def from_rows(left, right):
    return lax.dot_general(left, right, (((0,), (0,)), ((), ())), preferred_element_type=F32)


X_FIRST = (0, 1, 0, 0, 1, 0, 0, 1, 0, 1)
(
    SUM_ONE, SUM_TWO, SUM_THREE, SUM_LAST, WEIGHTS_Y, WEIGHTS_Z, WEIGHTS_LAST, ATTEND_BACK, ROWS_AWAY,
    ROWS_ACROSS, ROWS_HOME, NORM, EARLY_CORE, EARLY_X, EARLY_Z, EARLY_Y, EARLY_SHARE, EARLY_DONE, LATE_ROWS,
    LATE_DONE, BIAS_START, BIAS_NEXT, BIAS_DONE,
) = range(23)
BACKWARD_ORDER = (
    (SUM_ONE, 0), (SUM_ONE, 4), (SUM_ONE, 3), (SUM_ONE, 2), (SUM_ONE, 5), (EARLY_CORE, 0), (SUM_ONE, 1),
    (SUM_ONE, 6), (SUM_TWO, 0), (ATTEND_BACK, 3), (SUM_TWO, 3), (ATTEND_BACK, 1), (EARLY_X, 0), (SUM_ONE, 9),
    (ATTEND_BACK, 1), (SUM_TWO, 1), (ATTEND_BACK, 1), (SUM_TWO, 4), (SUM_THREE, 3), (SUM_THREE, 0),
    (ATTEND_BACK, 1), (EARLY_Z, 0), (SUM_TWO, 2), (SUM_TWO, 5), (SUM_ONE, 8), (SUM_TWO, 6), (ATTEND_BACK, 1),
    (SUM_ONE, 7), (SUM_THREE, 1), (ATTEND_BACK, 1), (SUM_TWO, 9), (EARLY_Y, 0), (SUM_THREE, 4), (SUM_THREE, 5),
    (ATTEND_BACK, 2), (SUM_THREE, 2), (SUM_THREE, 6), (ATTEND_BACK, 1), (SUM_THREE, 9), (SUM_TWO, 8),
    (SUM_TWO, 7), (ROWS_AWAY, 0), (WEIGHTS_Y, 0), (ROWS_ACROSS, 0), (SUM_THREE, 8), (SUM_THREE, 7),
    (WEIGHTS_Y, 2), (WEIGHTS_Z, 0), (BIAS_START, 0), (SUM_LAST, 3), (WEIGHTS_Y, 1), (ROWS_HOME, 0),
    (SUM_LAST, 5), (BIAS_NEXT, 0), (WEIGHTS_Z, 2), (WEIGHTS_Z, 1), (WEIGHTS_LAST, 0), (SUM_LAST, 8), (NORM, 0),
    (SUM_LAST, 2), (SUM_LAST, 1), (LATE_ROWS, 0), (SUM_LAST, 4), (BIAS_NEXT, 0), (WEIGHTS_LAST, 1),
    (BIAS_NEXT, 0), (EARLY_SHARE, 0), (WEIGHTS_LAST, 2), (LATE_DONE, 0), (SUM_LAST, 6), (SUM_LAST, 0),
    (EARLY_DONE, 0), (SUM_LAST, 7), (SUM_LAST, 9), (BIAS_DONE, 0),
)


def backward_kernel(
    depth,
    lens, do_in, qs_in, ks_in, vs_in, oh_in, lse_in, normed_in, wg_in, cos_in, sin_in, low, mods, frames, gmid,
    mg_in, bias_in, gwo, gup, gdown,
    fgrad, dwq, dwk, dwv, dwo, dup, ddown, dmw, mbias, btile,
    qs, do, oh, lse, normed, wg, cosr, sinr, ka, va, qaug, dk_sum, dv_sum, gr, gw, gwy, gwz, gsum,
    gnp, gnr, gnx, mod3, acc_shift, acc_scale, mg, mgr, mgs, mgx, ev, late, joined, ez, brecv, bz,
    *rest,
):
    send_sems, recv_sems, local_sems = rest[-3:]
    buffers = rest[:-3]
    here = Place(depth)
    z, y, x, c, g = here.z, here.y, here.x, here.c, here.seq
    span = frames.shape[0]
    rows_all = span * 4
    own_width = wg.shape[-1]
    move = Mover(send_sems, recv_sems, local_sems)
    steps_z = range(1, depth)

    shard, width = gwo.shape[4], MODEL_WIDTH
    thin = shard // 2
    pieces = []

    def add_piece(source, target, first_row, columns=None):
        rows = pl.ds(first_row, thin)
        if columns is None:
            pieces.append((source.at[:, :, :, :, rows], target.at[rows]))
        else:
            columns = pl.ds(columns, width)
            pieces.append((source.at[:, :, :, :, rows, columns], target.at[rows, columns]))

    for n in range(4):
        add_piece(gdown, ddown, n * thin)
    for n in range(2):
        add_piece(gup, dup, n * thin, 0)
        add_piece(gup, dup, n * thin, width)
    for n in range(2):
        add_piece(gwo, dwo, n * thin)
    count = len(pieces)
    own, first, second, third, fourth = (
        [buffers[count * n + f] for f in range(count)] for n in range(5)
    )
    legs = {}

    loads = [
        move.local(ks_in, ka.at[:, :, pl.ds(0, LANES)]),
        move.local(vs_in, va.at[:, :, pl.ds(0, LANES)]),
        move.local(qs_in, qs),
        move.local(do_in, do),
        move.local(oh_in, oh),
        move.local(lse_in, lse),
        move.local(cos_in, cosr),
        move.local(sin_in, sinr),
    ]
    here.enter(diagonal=True)
    held = []
    for f in range(count):
        source = pieces[f][0]
        legs[f] = move.send(source.at[:, :, :, 1 - c], first[f], here.core())
        held.append(move.local(source.at[:, :, :, c], own[f]))
    late_loads = [move.local(normed_in, normed), move.local(wg_in, wg)]

    def sum_first(f):
        legs[f].wait_recv()
        held[f].wait()

        def add(step, carry):
            own[f][step] = own[f][step] + first[f][step]
            return carry

        lax.fori_loop(0, depth, add, 0)
        if X_FIRST[f]:
            legs[f] = move.send(own[f].at[:, :, 1 - x], second[f], here.across_x())
        else:
            legs[f] = move.send(own[f].at[:, 1 - y], second[f], here.across_y())

    def sum_second(f):
        legs[f].wait_recv()

        def add(step, carry):
            for other in range(2):
                if X_FIRST[f]:
                    own[f][step, other, x] = own[f][step, other, x] + second[f][step, other]
                else:
                    own[f][step, y, other] = own[f][step, y, other] + second[f][step, other]
            return carry

        lax.fori_loop(0, depth, add, 0)
        if X_FIRST[f]:
            legs[f] = move.send(own[f].at[:, 1 - y, x], third[f], here.across_y())
        else:
            legs[f] = move.send(own[f].at[:, y, 1 - x], third[f], here.across_x())

    def sum_third(f):
        legs[f].wait_recv()

        def add(step, carry):
            own[f][step, y, x] = own[f][step, y, x] + third[f][step]
            return carry

        lax.fori_loop(0, depth, add, 0)
        legs[f] = [
            move.send(own[f].at[here.ahead(k), y, x], fourth[f].at[k - 1], here.along_z(k)) for k in steps_z
        ]

    def sum_last(f):
        total = own[f][z, y, x].astype(F32)
        for k in steps_z:
            legs[f][k - 1].wait_recv()
            total = total + fourth[f][k - 1].astype(F32)
        pieces[f][1][...] = total

    def bias_round(peer, slot):
        return move.send(btile, brecv.at[slot], peer)

    block = 128
    for copy in loads:
        copy.wait()

    def columns_of_segments(step, carry):
        rows = pl.ds(pl.multiple_of(step * block, block), block)
        segment, _ = frame_segments(lens, step * block, block, LANES)
        lane = lanes_of((block, LANES))
        same = segment == lane
        qaug[rows, :] = jnp.where((lane < SEGS) & jnp.logical_not(same), NEGATIVE, 0.0).astype(BF16)
        keyside = jnp.where((lane < SEGS) & same, 1.0, jnp.where((lane >= 4) & (lane < 7), 1.0, 0.0))
        for pair in range(2):
            ka[pair, rows, LANES:] = keyside.astype(BF16)
            va[pair, rows, LANES:] = jnp.where(lane < 3, 1.0, 0.0).astype(BF16)
        return carry

    lax.fori_loop(0, rows_all // block, columns_of_segments, 0)

    tall = 256
    steps = rows_all // tall

    def back_block(pair, step):
        rows = pl.ds(pl.multiple_of(step * tall, tall), tall)
        lane = lanes_of((tall, LANES))
        query, given = qs[pair, rows, :], do[pair, rows, :]
        overlap = given.astype(F32) * oh[pair, rows, :].astype(F32)
        mask_columns = qaug[rows, :].astype(F32)
        sums = lse[rows, :]
        grads_q, add_k, add_v = [], 0.0, 0.0
        for head in range(2):
            delta = jnp.sum(jnp.where((lane >= HEAD_DIM) == bool(head), overlap, 0.0), axis=1, keepdims=True)
            logsum = jnp.sum(jnp.where(lane == 2 * pair + head, sums, 0.0), axis=1, keepdims=True)
            a, b, d = three_parts(logsum)
            side = jnp.where(lane == 4, -a, jnp.where(lane == 5, -b, jnp.where(lane == 6, -d, mask_columns)))
            query_head = head_only(query, lane, head)
            left = jnp.concatenate([query_head, side.astype(BF16)], axis=1)
            a, b, d = three_parts(delta)
            side = jnp.where(lane == 0, -a, jnp.where(lane == 1, -b, jnp.where(lane == 2, -d, 0.0)))
            given_head = head_only(given, lane, head)
            right = jnp.concatenate([given_head, side.astype(BF16)], axis=1)
            weights = jnp.exp(across(ka[pair], left))
            grads = (weights * across(va[pair], right)).astype(BF16)
            add_v = add_v + product(weights.astype(BF16), given_head)
            add_k = add_k + product(grads, query_head)
            grads_q.append(from_rows(grads, ka[pair, :, :LANES]))
        dv_sum[...] += add_v
        dk_sum[...] += add_k
        grad_query = jnp.where(lane < HEAD_DIM, grads_q[0], grads_q[1]) * HEAD_DIM**-0.5
        gr[0, rows, pair * LANES : (pair + 1) * LANES] = turn_back(
            grad_query, cosr[rows, :], sinr[rows, :], lane
        ).astype(BF16)

    def back_some(pair, start, stop):
        lax.fori_loop(start, stop, lambda step, carry: (back_block(pair, step), carry)[1], 0)

    def settle_pair(pair):
        def body(step, carry):
            rows = pl.ds(pl.multiple_of(step * block, block), block)
            lane = lanes_of((block, LANES))
            part = slice(pair * LANES, (pair + 1) * LANES)
            gr[1, rows, part] = turn_back(dk_sum[rows, :], cosr[rows, :], sinr[rows, :], lane).astype(BF16)
            gr[2, rows, part] = dv_sum[rows, :].astype(BF16)
            return carry

        lax.fori_loop(0, rows_all // block, body, 0)

    def clear():
        dk_sum[...] = jnp.zeros_like(dk_sum)
        dv_sum[...] = jnp.zeros_like(dv_sum)

    def back_rows(target):
        def body(step, carry):
            rows = pl.ds(pl.multiple_of(target * span + step * block, block), block)
            total = 0.0
            for j in range(3):
                total = total + across(gr[j, rows, :], wg[j].reshape(MODEL_WIDTH, own_width))
            gnp[target, pl.ds(pl.multiple_of(step * block, block), block), :] = total.astype(BF16)
            return carry

        lax.fori_loop(0, span // block, body, 0)

    away_other, away_same = (1 - x) * 2 + (1 - c), (1 - x) * 2 + c
    home_other = x * 2 + (1 - c)
    gn = {}

    def rows_away():
        for copy in late_loads:
            copy.wait()
        back_rows(away_other)
        gn["core"] = move.send(gnp.at[away_other], gnr.at[0], here.core())

    def rows_across():
        back_rows(away_same)
        gn["core"].wait_recv()

        def add_rows(step, carry):
            rows = pl.ds(pl.multiple_of(step * block, block), block)
            gnp[away_same, rows, :] = gnp[away_same, rows, :] + gnr[0, rows, :]
            return carry

        lax.fori_loop(0, span // block, add_rows, 0)
        gn["x"] = move.send(gnp.at[away_same], gnx, here.across_x())

    def rows_home():
        back_rows(home_other)
        gn["home"] = move.send(gnp.at[home_other], gnr.at[1], here.core())
        back_rows(g)

    tile = 256

    def weight_rows(j):
        def body(step, carry):
            columns = pl.ds(pl.multiple_of(step * tile, tile), tile)
            result = from_rows(normed[:, columns], gr[j]).astype(BF16)
            per = 2 * 4 * shard // tile
            lead = result.reshape(tile // (4 * shard), 4, shard, own_width)
            for n in range(tile // (4 * shard)):
                gw[j, step // per, (step % per) * (tile // (4 * shard)) + n] = lead[n]
            return carry

        lax.fori_loop(0, MODEL_WIDTH // tile, body, 0)

    gw_y, gw_z = {}, {}

    def weights_y(j):
        weight_rows(j)
        gw_y[j] = move.send(gw.at[j, :, 1 - y], gwy.at[j], here.across_y())

    def weights_z(j):
        gw_y[j].wait_recv()

        def add(step, carry):
            gw[j, step, y] = gw[j, step, y] + gwy[j, step]
            return carry

        lax.fori_loop(0, depth, add, 0)
        gw_z[j] = [move.send(gw.at[j, here.ahead(k), y], gwz.at[j, k - 1], here.along_z(k)) for k in steps_z]

    outs = (dwq, dwk, dwv)
    final = []
    final_locals = []

    def weights_last(j):
        total = gw[j, z, y].astype(F32)
        for k in steps_z:
            gw_z[j][k - 1].wait_recv()
            total = total + gwz[j, k - 1].astype(F32)
        gsum[j] = total
        columns = pl.ds(pl.multiple_of(g * own_width, LANES), own_width)
        final_locals.append(move.local(gsum.at[j, g], outs[j].at[:, columns]))
        for k in (1, 2, 3):
            final.append(move.send(gsum.at[j, (g + k) % 4], outs[j].at[:, columns], here.row_peer(k)))

    bias_legs = []

    def bias_start():
        ones = jnp.ones((16, rows_all), BF16)
        btile[...] = bias_in[...]
        for j in range(3):
            sums = product(ones, gr[j])
            for half in range(2):
                btile[pl.ds(8 * j + g * 2 + half, 1), :] = sums[0:1, half * LANES : (half + 1) * LANES]
        bias_legs.append(move.send(btile, brecv.at[0], here.core()))

    def bias_next():
        done = len(bias_legs)
        bias_legs[-1].wait()
        btile[...] = btile[...] + brecv[done - 1]
        if done < 3:
            peer = (here.across_x, here.across_y)[done - 1]()
            bias_legs.append(move.send(btile, brecv.at[done], peer))
        else:
            bias_legs.extend([move.send(btile, bz.at[k - 1], here.along_z(k)) for k in steps_z])

    def bias_last():
        for copy in bias_legs[3:]:
            copy.wait()
        total = btile[...]
        for k in steps_z:
            total = total + bz[k - 1]
        btile[...] = total

    high, middle, rest_part = three_parts(mods[0:4, MODEL_WIDTH : 2 * MODEL_WIDTH])
    mod3[0:4, :] = high
    mod3[4:8, :] = middle
    mod3[8:12, :] = rest_part
    mod3[12:16, :] = jnp.zeros((4, MODEL_WIDTH), F32)
    acc_shift[...] = jnp.zeros_like(acc_shift)
    acc_scale[...] = jnp.zeros_like(acc_scale)
    def two_parts(values):
        top = values.astype(BF16)
        return top, (values - top.astype(F32)).astype(BF16)

    def norm_rows(step, carry):
        rows = pl.ds(pl.multiple_of(step * block, block), block)
        grad = gnp[g, rows, :].astype(F32) + gnr[1, rows, :].astype(F32) + gnx[rows, :].astype(F32)
        values = frames[rows, :].astype(F32)
        center = jnp.mean(values, axis=1, keepdims=True)
        centered = values - center
        scaled = lax.rsqrt(jnp.mean(centered * centered, axis=1, keepdims=True) + EPSILON)
        hat = centered * scaled
        base = g * span + step * block
        segment, _ = frame_segments(lens, base, block, 16)
        slot = lanes_of((block, 16))
        chosen = jnp.where((slot < 12) & (slot % 4 == segment), 1.0, 0.0).astype(BF16)
        inner = grad * (1.0 + product(chosen, mod3[...].astype(BF16)))
        mean_one = jnp.mean(inner, axis=1, keepdims=True)
        mean_two = jnp.mean(inner * hat, axis=1, keepdims=True)
        fgrad[rows, :] = (gmid[rows, :] + scaled * (inner - mean_one - hat * mean_two)).astype(BF16)
        position = base + lanes_of((16, block))
        begin = [lens[0, 0], lens[0, 0] + lens[0, 1], lens[0, 0] + lens[0, 1] + lens[0, 2]]
        inside = sum((position >= edge).astype(jnp.int32) for edge in begin)
        members = jnp.where(inside == lanes_of((16, block), 0), 1.0, 0.0).astype(BF16)
        for values, target in ((grad, acc_shift), (grad * hat, acc_scale)):
            top, bottom = two_parts(values)
            target[...] += product(members, top) + product(members, bottom)
        return carry

    fourth_part = MODEL_WIDTH // 2
    mod_legs = {}

    def mods_core():
        for side in range(2):
            mg[side] = mg_in[:, side * fourth_part : (side + 1) * fourth_part]
        mod_legs["core"] = move.send(mg.at[1 - c], mgr, here.core())

    def mods_x():
        mod_legs["core"].wait_recv()
        mgs[...] = mg[c] + mgr[...]
        mod_legs["x"] = move.send(mgs, mgx, here.across_x())

    def mods_z():
        mod_legs["x"].wait_recv()
        ev[z, y, c] = (mgs[...] + mgx[...]).astype(BF16)
        mod_legs["z"] = [move.send(ev.at[z, y, c], ev.at[z, y, c], here.along_z(k)) for k in steps_z]

    def mods_y():
        for copy in mod_legs["z"]:
            copy.wait_recv()
        mod_legs["y"] = move.send(ev.at[:, y, c], ev.at[:, y, c], here.across_y())

    def mods_share():
        mod_legs["y"].wait_recv()
        mod_legs["last"] = move.send(ev.at[:, :, c], ev.at[:, :, c], here.core())

    every_row = 32 * depth
    picks = jnp.where(
        lanes_of((16, every_row), 0) == (lanes_of((16, every_row)) % 16) // 4, 1.0, 0.0
    ).astype(BF16)

    def place_columns(every, start, stride):
        size = every.shape[1]
        result = from_rows(low[...], every)
        summed = product(picks, every)
        for strip in range(4):
            columns = slice(start + strip * stride, start + strip * stride + size)
            dmw[:, columns] = result[32 * strip : 32 * (strip + 1), :]
            mbias[0:1, columns] = summed[strip : strip + 1, :]

    def mods_early():
        mod_legs["last"].wait_recv()
        for side in range(2):
            every = ev[:, :, side].reshape(every_row, fourth_part)
            place_columns(every, 2 * MODEL_WIDTH + side * fourth_part, MODEL_WIDTH)

    def norm_part():
        gn["home"].wait_recv()
        gn["x"].wait_recv()
        lax.fori_loop(0, span // block, norm_rows, 0)
        late[0, 0:4, :] = acc_shift[0:4, :]
        late[0, 4:8, :] = acc_scale[0:4, :]
        mod_legs["row"] = [move.send(late.at[0], late.at[k], here.row_peer(k)) for k in (1, 2, 3)]

    def mods_rows():
        for copy in mod_legs["row"]:
            copy.wait_recv()
        total = (late[0] + late[1]) + (late[2] + late[3])
        joined[0:4, :] = total[0:4, :fourth_part]
        joined[4:8, :] = total[0:4, fourth_part:]
        joined[8:12, :] = total[4:8, :fourth_part]
        joined[12:16, :] = total[4:8, fourth_part:]
        ez[z, y] = joined[...].astype(BF16)
        peers = [here.along_z(k) for k in steps_z] + [here.across_y()]
        peers += [here.at(here.ahead(k), 1 - y, x, c) for k in steps_z]
        mod_legs["all"] = [move.send(ez.at[z, y], ez.at[z, y], peer) for peer in peers]

    def mods_late():
        for copy in mod_legs["all"]:
            copy.wait_recv()
        place_columns(ez[...].reshape(every_row, fourth_part), 0, fourth_part)

    stages = {
        SUM_ONE: sum_first, SUM_TWO: sum_second, SUM_THREE: sum_third, SUM_LAST: sum_last,
        WEIGHTS_Y: weights_y, WEIGHTS_Z: weights_z, WEIGHTS_LAST: weights_last,
    }
    others = {
        ROWS_AWAY: rows_away, ROWS_ACROSS: rows_across, ROWS_HOME: rows_home, NORM: norm_part,
        EARLY_CORE: mods_core, EARLY_X: mods_x, EARLY_Z: mods_z, EARLY_Y: mods_y, EARLY_SHARE: mods_share, EARLY_DONE: mods_early,
        LATE_ROWS: mods_rows, LATE_DONE: mods_late, BIAS_START: bias_start, BIAS_NEXT: bias_next, BIAS_DONE: bias_last,
    }
    clear()
    done = 0
    for code, number in BACKWARD_ORDER:
        if code == ATTEND_BACK:
            ahead = number
            while ahead:
                pair, at = done // steps, done % steps
                now = min(ahead, steps - at)
                back_some(pair, at, at + now)
                done, ahead = done + now, ahead - now
                if done % steps == 0:
                    settle_pair(pair)
                    if pair == 0:
                        clear()
        elif code in others:
            others[code]()
        else:
            stages[code](number)
    for copy in final_locals:
        copy.wait()
    for copy in final:
        copy.wait_recv()
    move.finish(but=bias_legs)


def backward_call(depth, span, own_rows, down_rows, hidden, args):
    rows_all, own_width = 4 * span, MODEL_WIDTH // 4
    half = MODEL_WIDTH // 2
    vmem, anywhere, scalar = (
        pl.BlockSpec(memory_space=pltpu.VMEM),
        pl.BlockSpec(memory_space=pl.ANY),
        pl.BlockSpec(memory_space=pltpu.SMEM),
    )

    def out(shape, dtype):
        return jax.ShapeDtypeStruct(shape, dtype)

    outs = [
        (out((span, MODEL_WIDTH), BF16), vmem),
        (out((own_rows, MODEL_WIDTH), F32), anywhere),
        (out((own_rows, MODEL_WIDTH), F32), anywhere),
        (out((own_rows, MODEL_WIDTH), F32), anywhere),
        (out((own_rows, MODEL_WIDTH), F32), vmem),
        (out((own_rows, hidden), F32), vmem),
        (out((down_rows, MODEL_WIDTH), F32), vmem),
        (out((own_rows, 6 * MODEL_WIDTH), F32), vmem),
        (out((8, 6 * MODEL_WIDTH), F32), vmem),
        (out((56, LANES), F32), vmem),
    ]
    pair_rows = pltpu.VMEM((2, rows_all, LANES), BF16)
    wide_rows = pltpu.VMEM((2, rows_all, 2 * LANES), BF16)
    table = pltpu.VMEM((rows_all, LANES), F32)
    scratch = [
        pair_rows, pair_rows, pair_rows, table,
        pltpu.VMEM((rows_all, MODEL_WIDTH), BF16),
        pltpu.VMEM((3, depth, 2, 4, own_rows, own_width), BF16),
        table, table, wide_rows, wide_rows,
        pltpu.VMEM((rows_all, LANES), BF16),
        table, table,
        pltpu.VMEM((3, rows_all, own_width), BF16),
        pltpu.VMEM((3, depth, 2, 4, own_rows, own_width), BF16),
        pltpu.VMEM((3, depth, 4, own_rows, own_width), BF16),
        pltpu.VMEM((3, depth - 1, 4, own_rows, own_width), BF16),
        pltpu.VMEM((3, 4, own_rows, own_width), F32),
        pltpu.VMEM((4, span, MODEL_WIDTH), BF16),
        pltpu.VMEM((2, span, MODEL_WIDTH), BF16),
        pltpu.VMEM((span, MODEL_WIDTH), BF16),
        pltpu.VMEM((16, MODEL_WIDTH), F32),
        pltpu.VMEM((16, MODEL_WIDTH), F32),
        pltpu.VMEM((16, MODEL_WIDTH), F32),
        pltpu.VMEM((2, 16, half), F32),
        pltpu.VMEM((16, half), F32),
        pltpu.VMEM((16, half), F32),
        pltpu.VMEM((16, half), F32),
        pltpu.VMEM((depth, 2, 2, 16, half), BF16),
        pltpu.VMEM((4, 8, MODEL_WIDTH), F32),
        pltpu.VMEM((16, half), F32),
        pltpu.VMEM((depth, 2, 16, half), BF16),
        pltpu.VMEM((3, 56, LANES), F32),
        pltpu.VMEM((depth - 1, 56, LANES), F32),
    ]
    piece = (own_rows // 2, MODEL_WIDTH)
    for lead in ((depth, 2, 2), (depth, 2, 2), (depth, 2), (depth,), (depth - 1,)):
        scratch += [pltpu.VMEM(lead + piece, BF16)] * 10
    scratch += [pltpu.SemaphoreType.DMA((128,)), pltpu.SemaphoreType.DMA((128,)), pltpu.SemaphoreType.DMA((32,))]
    return pl.pallas_call(
        partial(backward_kernel, depth),
        out_shape=[shape for shape, _ in outs],
        in_specs=[scalar] + [anywhere] * 10 + [vmem] * 6 + [anywhere] * 3,
        out_specs=[spec for _, spec in outs],
        scratch_shapes=scratch,
        compiler_params=pltpu.CompilerParams(
            collective_id=1, has_side_effects=True, vmem_limit_bytes=62 * 1024 * 1024
        ),
        cost_estimate=pl.CostEstimate(flops=2 * 10**10, bytes_accessed=40 * 10**6, transcendentals=10**7),
    )(*args)


def modulated_norm(values, shift_part, scale_part):
    center = jnp.mean(values, axis=-1, keepdims=True)
    centered = values - center
    variance = jnp.mean(centered * centered, axis=-1, keepdims=True)
    return centered * lax.rsqrt(variance + EPSILON) * (1.0 + scale_part) + shift_part


def rotate(values, cosines, sines_table):
    shaped = values.reshape(values.shape[:-1] + (values.shape[-1] // HEAD_DIM, HEAD_DIM))
    first_half = shaped[..., : HEAD_DIM // 2]
    second_half = shaped[..., HEAD_DIM // 2 :]
    cosine = cosines[..., None, :]
    sine_part = sines_table[..., None, :]
    turned = jnp.concatenate(
        [
            first_half * cosine - second_half * sine_part,
            second_half * cosine + first_half * sine_part,
        ],
        axis=-1,
    )
    return turned.reshape(values.shape)


def gelu_tanh(values):
    return jax.nn.gelu(values, approximate=True)


def time_features(time_index):
    halfway = MODEL_WIDTH // 2
    frequency = jnp.exp(jnp.arange(halfway, dtype=jnp.float32) * (-math.log(10000.0) / halfway))
    angles = time_index.astype(jnp.float32)[..., None] * frequency
    return jnp.concatenate([jnp.sin(angles), jnp.cos(angles)], axis=-1)


def segment_starts(segment_lengths):
    return jnp.cumsum(segment_lengths, axis=1) - segment_lengths


def segment_numbers(segment_lengths, frame_positions):
    starts = segment_starts(segment_lengths)
    inside = (frame_positions[None, :, None] >= starts[:, None, :]).astype(jnp.int32)
    return jnp.sum(inside, axis=2) - 1


def segment_layout(segment_lengths, frame_positions):
    starts = segment_starts(segment_lengths)
    segment = segment_numbers(segment_lengths, frame_positions)
    onehot = (segment[..., None] == jnp.arange(SEGS, dtype=jnp.int32)).astype(jnp.float32)
    offset = jnp.sum(onehot * starts[:, None, :].astype(jnp.float32), axis=2)
    relative = frame_positions[None, :].astype(jnp.float32) - offset
    return (onehot, relative)


def rope_tables(relative):
    halfway = HEAD_DIM // 2
    frequency = jnp.exp(jnp.arange(halfway, dtype=jnp.float32) * (-math.log(10000.0) / halfway))
    angles = relative[..., None] * frequency
    return (jnp.cos(angles), jnp.sin(angles))


def project(values, matrix, offset):
    return jnp.einsum(
        "rld,de->rle", values, matrix, preferred_element_type=jnp.float32
    ) + offset.astype(jnp.float32)


def project_back(gradient, matrix):
    return jnp.einsum("rle,de->rld", gradient, matrix, preferred_element_type=jnp.float32)


def weight_gradient(values, gradient):
    return jnp.einsum("rld,rle->de", values, gradient, preferred_element_type=jnp.float32)


def bias_gradient(gradient):
    return jnp.sum(gradient.astype(jnp.float32), axis=(0, 1))


def lift_up(member):
    return member.reshape((1, 1) + member.shape)


def settle(member):
    return member.reshape((-1,) + member.shape[3:])


def spread(member, wide_count, narrow_count):
    return member.reshape((wide_count, narrow_count, -1) + member.shape[1:])


def unpack(member):
    return member.reshape(member.shape[2:])


def on_device(
    frames,
    output_gradient,
    segment_lengths,
    time_index,
    query_weight,
    query_bias,
    key_weight,
    key_bias,
    value_weight,
    value_bias,
    output_projection,
    output_bias,
    up_weight,
    up_bias,
    down_weight,
    down_bias,
    modulation_weight,
    modulation_bias,
):
    narrow_count = lax.axis_size("seq")
    wide_count = lax.axis_size("dp")
    seq_index = lax.axis_index("seq")
    row_count, span_frames, width_total = frames.shape
    row_length = span_frames * narrow_count
    block_rows = min(512, row_length)
    block_count = row_length // block_rows
    local_weights = (
        query_weight,
        query_bias,
        key_weight,
        key_bias,
        value_weight,
        value_bias,
        output_projection,
        output_bias,
        up_weight,
        up_bias,
        down_weight,
        down_bias,
        modulation_bias,
    )
    lifted = [lift_up(member) for member in local_weights]
    halfway_set = (
        lax.all_gather(lifted[0], "dp", axis=0, tiled=True),
        lax.all_gather(lifted[1], "dp", axis=0, tiled=True),
        lax.all_gather(lifted[2], "dp", axis=0, tiled=True),
        lax.all_gather(lifted[3], "dp", axis=0, tiled=True),
        lax.all_gather(lifted[4], "dp", axis=0, tiled=True),
        lax.all_gather(lifted[5], "dp", axis=0, tiled=True),
        lax.all_gather(lifted[6], "dp", axis=0, tiled=True),
        lax.all_gather(lifted[7], "dp", axis=0, tiled=True),
        lax.all_gather(lifted[8], "dp", axis=0, tiled=True),
        lax.all_gather(lifted[9], "dp", axis=0, tiled=True),
        lax.all_gather(lifted[10], "dp", axis=0, tiled=True),
        lax.all_gather(lifted[11], "dp", axis=0, tiled=True),
        lax.all_gather(lifted[12], "dp", axis=0, tiled=True),
    )
    complete_set = (
        lax.all_gather(halfway_set[0], "seq", axis=1, tiled=True),
        lax.all_gather(halfway_set[1], "seq", axis=1, tiled=True),
        lax.all_gather(halfway_set[2], "seq", axis=1, tiled=True),
        lax.all_gather(halfway_set[3], "seq", axis=1, tiled=True),
        lax.all_gather(halfway_set[4], "seq", axis=1, tiled=True),
        lax.all_gather(halfway_set[5], "seq", axis=1, tiled=True),
        lax.all_gather(halfway_set[6], "seq", axis=1, tiled=True),
        lax.all_gather(halfway_set[7], "seq", axis=1, tiled=True),
        lax.all_gather(halfway_set[8], "seq", axis=1, tiled=True),
        lax.all_gather(halfway_set[9], "seq", axis=1, tiled=True),
        lax.all_gather(halfway_set[10], "seq", axis=1, tiled=True),
        lax.all_gather(halfway_set[11], "seq", axis=1, tiled=True),
        lax.all_gather(halfway_set[12], "seq", axis=1, tiled=True),
    )
    gathered = [settle(member) for member in complete_set]
    (
        full_query,
        full_query_bias,
        full_key,
        full_key_bias,
        full_value,
        full_value_bias,
        full_output,
        full_output_bias,
        full_up,
        full_up_bias,
        full_down,
        full_down_bias,
        full_modulation_bias,
    ) = gathered
    local_positions = seq_index * span_frames + jnp.arange(span_frames, dtype=jnp.int32)
    local_onehot, local_relative = segment_layout(segment_lengths, local_positions)
    row_segment = segment_numbers(segment_lengths, jnp.arange(row_length, dtype=jnp.int32))
    cosines, sines_table = rope_tables(local_relative)
    turning = partial(rotate, cosines=cosines, sines_table=sines_table)
    owned_rows = modulation_weight.shape[0]
    owned_start = (lax.axis_index("dp") * narrow_count + seq_index) * owned_rows
    every_time = lax.all_gather(time_index, "dp", axis=0, tiled=True)
    every_low = jax.nn.silu(time_features(every_time)).astype(jnp.bfloat16)
    owned_low = lax.dynamic_slice_in_dim(every_low, owned_start, owned_rows, 2)
    partial_modulation = jnp.einsum(
        "rsd,dc->rsc", owned_low, modulation_weight, preferred_element_type=jnp.float32
    )
    row_share = lax.psum_scatter(partial_modulation, "dp", scatter_dimension=0, tiled=True)
    modulation = lax.psum(row_share.astype(jnp.bfloat16), "seq").astype(
        jnp.float32
    ) + full_modulation_bias.astype(jnp.float32)
    per_frame = jnp.einsum("rls,rsc->rlc", local_onehot, modulation, precision=HIGHEST)
    shift_one, scale_one, gate_one, shift_two, scale_two, gate_two = jnp.split(
        per_frame, 6, axis=-1
    )
    inputs = frames.astype(jnp.float32)
    normed, norm_back = jax.vjp(modulated_norm, inputs, shift_one, scale_one)
    normed_low = normed.astype(jnp.bfloat16)
    query_pre = project(normed_low, full_query, full_query_bias)
    key_pre = project(normed_low, full_key, full_key_bias)
    value_low = project(normed_low, full_value, full_value_bias).astype(jnp.bfloat16)
    query_turned, query_back = jax.vjp(turning, query_pre)
    key_turned, key_back = jax.vjp(turning, key_pre)
    query_heads, key_heads, value_heads = (
        lax.all_to_all(
            query_turned.astype(jnp.bfloat16), "seq", split_axis=2, concat_axis=1, tiled=True
        ),
        lax.all_to_all(
            key_turned.astype(jnp.bfloat16), "seq", split_axis=2, concat_axis=1, tiled=True
        ),
        lax.all_to_all(value_low, "seq", split_axis=2, concat_axis=1, tiled=True),
    )
    local_heads = query_heads.shape[2] // HEAD_DIM
    head_shape = (row_count, row_length, local_heads, HEAD_DIM)
    queries = query_heads.reshape(head_shape)
    keys_all = key_heads.reshape(head_shape)
    values_all = value_heads.reshape(head_shape)
    scaling = HEAD_DIM ** (-0.5)
    positions_all = jnp.arange(row_count * block_count, dtype=jnp.int32)

    def fetch_block(position):
        row_index = position // block_count
        start_row = position % block_count * block_rows
        key_row = lax.dynamic_index_in_dim(keys_all, row_index, 0, keepdims=False)
        value_row = lax.dynamic_index_in_dim(values_all, row_index, 0, keepdims=False)
        segment_row = lax.dynamic_index_in_dim(row_segment, row_index, 0, keepdims=False)
        query_block = lax.dynamic_slice_in_dim(
            lax.dynamic_index_in_dim(queries, row_index, 0, keepdims=False),
            start_row,
            block_rows,
            0,
        )
        segment_block = lax.dynamic_slice_in_dim(segment_row, start_row, block_rows, 0)
        scores = (
            jnp.einsum("bhd,khd->hbk", query_block, key_row, preferred_element_type=jnp.float32)
            * scaling
        )
        scores = jnp.where((segment_block[:, None] == segment_row[None, :])[None], scores, NEGATIVE)
        return (row_index, start_row, query_block, key_row, value_row, scores)

    def forward_block(position):
        row_index, start_row, query_block, key_row, value_row, scores = fetch_block(position)
        highest = jnp.max(scores, axis=2, keepdims=True)
        weights = jnp.exp(scores - highest)
        totals = jnp.sum(weights, axis=2, keepdims=True)
        probabilities = (weights / totals).astype(jnp.bfloat16)
        mixed_block = jnp.einsum(
            "hbk,khd->bhd", probabilities, value_row, preferred_element_type=jnp.float32
        )
        return (
            mixed_block.astype(jnp.bfloat16).reshape(block_rows, -1),
            (highest + jnp.log(totals))[..., 0],
        )

    mixed_blocks, logsums = lax.map(forward_block, positions_all)
    attention_heads = mixed_blocks.reshape(row_count, row_length, -1)
    attention_frames = lax.all_to_all(
        attention_heads, "seq", split_axis=1, concat_axis=2, tiled=True
    )
    branch = project(attention_frames, full_output, full_output_bias)
    middle = inputs + gate_one * branch
    normed_two, norm_two_back = jax.vjp(modulated_norm, middle, shift_two, scale_two)
    normed_two_low = normed_two.astype(jnp.bfloat16)
    hidden = project(normed_two_low, full_up, full_up_bias)
    activated, gelu_back = jax.vjp(gelu_tanh, hidden)
    activated_low = activated.astype(jnp.bfloat16)
    branch_two = project(activated_low, full_down, full_down_bias)
    layer_output = (middle + gate_two * branch_two).astype(jnp.bfloat16)
    cotangent = output_gradient.astype(jnp.float32)
    grad_branch_two = (gate_two * cotangent).astype(jnp.bfloat16)
    grad_gate_two = cotangent * branch_two
    grad_activated = project_back(grad_branch_two, full_down)
    grad_hidden = gelu_back(grad_activated)[0].astype(jnp.bfloat16)
    grad_normed_two = project_back(grad_hidden, full_up)
    grad_middle_part, grad_shift_two, grad_scale_two = norm_two_back(grad_normed_two)
    grad_middle = cotangent + grad_middle_part
    grad_gate_one = grad_middle * branch
    grad_branch = (gate_one * grad_middle).astype(jnp.bfloat16)
    grad_attention = project_back(grad_branch, full_output).astype(jnp.bfloat16)
    grad_heads = lax.all_to_all(grad_attention, "seq", split_axis=2, concat_axis=1, tiled=True)
    grad_outputs = grad_heads.reshape(head_shape)

    def backward_block(running, pair_inputs):
        grad_keys, grad_values = running
        position, logsum = pair_inputs
        row_index, start_row, query_block, key_row, value_row, scores = fetch_block(position)
        grad_block = lax.dynamic_slice_in_dim(
            lax.dynamic_index_in_dim(grad_outputs, row_index, 0, keepdims=False),
            start_row,
            block_rows,
            0,
        )
        probabilities = jnp.exp(scores - logsum[..., None])
        grad_probabilities = jnp.einsum(
            "bhd,khd->hbk", grad_block, value_row, preferred_element_type=jnp.float32
        )
        delta_sum = jnp.sum(probabilities * grad_probabilities, axis=2, keepdims=True)
        grad_scores = (probabilities * (grad_probabilities - delta_sum)).astype(jnp.bfloat16)
        grad_query_block = (
            jnp.einsum("hbk,khd->bhd", grad_scores, key_row, preferred_element_type=jnp.float32)
            * scaling
        )
        key_part = (
            jnp.einsum("hbk,bhd->khd", grad_scores, query_block, preferred_element_type=jnp.float32)
            * scaling
        )
        value_part = jnp.einsum(
            "hbk,bhd->khd",
            probabilities.astype(jnp.bfloat16),
            grad_block,
            preferred_element_type=jnp.float32,
        )
        grad_keys = lax.dynamic_update_index_in_dim(
            grad_keys,
            lax.dynamic_index_in_dim(grad_keys, row_index, 0, keepdims=False) + key_part,
            row_index,
            0,
        )
        grad_values = lax.dynamic_update_index_in_dim(
            grad_values,
            lax.dynamic_index_in_dim(grad_values, row_index, 0, keepdims=False) + value_part,
            row_index,
            0,
        )
        return (
            (grad_keys, grad_values),
            grad_query_block.astype(jnp.bfloat16).reshape(block_rows, -1),
        )

    zero_heads = jnp.zeros(head_shape, jnp.float32)
    (grad_keys_all, grad_values_all), grad_query_blocks = lax.scan(
        backward_block, (zero_heads, zero_heads), (positions_all, logsums)
    )
    flat_shape = (row_count, row_length, -1)
    grad_query_frames, grad_key_frames, grad_value_frames = (
        lax.all_to_all(
            grad_query_blocks.reshape(flat_shape), "seq", split_axis=1, concat_axis=2, tiled=True
        ),
        lax.all_to_all(
            grad_keys_all.reshape(flat_shape).astype(jnp.bfloat16),
            "seq",
            split_axis=1,
            concat_axis=2,
            tiled=True,
        ),
        lax.all_to_all(
            grad_values_all.reshape(flat_shape).astype(jnp.bfloat16),
            "seq",
            split_axis=1,
            concat_axis=2,
            tiled=True,
        ),
    )
    grad_query_pre = query_back(grad_query_frames.astype(jnp.float32))[0].astype(jnp.bfloat16)
    grad_key_pre = key_back(grad_key_frames.astype(jnp.float32))[0].astype(jnp.bfloat16)
    grad_normed = (
        project_back(grad_query_pre, full_query)
        + project_back(grad_key_pre, full_key)
        + project_back(grad_value_frames, full_value)
    )
    grad_inputs_part, grad_shift_one, grad_scale_one = norm_back(grad_normed)
    frames_grad = (grad_middle + grad_inputs_part).astype(jnp.bfloat16)
    grad_per_frame = jnp.concatenate(
        [
            grad_shift_one,
            grad_scale_one,
            grad_gate_one,
            grad_shift_two,
            grad_scale_two,
            grad_gate_two,
        ],
        axis=-1,
    )
    grad_modulation = jnp.einsum("rls,rlc->rsc", local_onehot, grad_per_frame, precision=HIGHEST)
    gradients = (
        weight_gradient(normed_low, grad_query_pre),
        bias_gradient(grad_query_pre),
        weight_gradient(normed_low, grad_key_pre),
        bias_gradient(grad_key_pre),
        weight_gradient(normed_low, grad_value_frames),
        bias_gradient(grad_value_frames),
        weight_gradient(attention_frames, grad_branch),
        bias_gradient(grad_branch),
        weight_gradient(normed_two_low, grad_hidden),
        bias_gradient(grad_hidden),
        weight_gradient(activated_low, grad_branch_two),
        bias_gradient(grad_branch_two),
        jnp.sum(grad_modulation, axis=(0, 1)),
    )
    row_total = lax.psum(grad_modulation.astype(jnp.bfloat16), "seq").astype(jnp.float32)
    every_grad = lax.all_gather(row_total.astype(jnp.bfloat16), "dp", axis=0, tiled=True).astype(
        row_total.dtype
    )
    modulation_weight_grad = jnp.einsum(
        "rsd,rsc->dc", owned_low.astype(jnp.float32), every_grad, precision=HIGHEST
    )
    spreaded = [spread(member, wide_count, narrow_count) for member in gradients]
    first_pass = (
        lax.psum_scatter(
            spreaded[0].astype(jnp.bfloat16), "seq", scatter_dimension=1, tiled=True
        ).astype(jnp.float32),
        lax.psum_scatter(
            spreaded[1].astype(jnp.bfloat16), "seq", scatter_dimension=1, tiled=True
        ).astype(jnp.float32),
        lax.psum_scatter(
            spreaded[2].astype(jnp.bfloat16), "seq", scatter_dimension=1, tiled=True
        ).astype(jnp.float32),
        lax.psum_scatter(
            spreaded[3].astype(jnp.bfloat16), "seq", scatter_dimension=1, tiled=True
        ).astype(jnp.float32),
        lax.psum_scatter(
            spreaded[4].astype(jnp.bfloat16), "seq", scatter_dimension=1, tiled=True
        ).astype(jnp.float32),
        lax.psum_scatter(
            spreaded[5].astype(jnp.bfloat16), "seq", scatter_dimension=1, tiled=True
        ).astype(jnp.float32),
        lax.psum_scatter(
            spreaded[6].astype(jnp.bfloat16), "seq", scatter_dimension=1, tiled=True
        ).astype(jnp.float32),
        lax.psum_scatter(
            spreaded[7].astype(jnp.bfloat16), "seq", scatter_dimension=1, tiled=True
        ).astype(jnp.float32),
        lax.psum_scatter(
            spreaded[8].astype(jnp.bfloat16), "seq", scatter_dimension=1, tiled=True
        ).astype(jnp.float32),
        lax.psum_scatter(
            spreaded[9].astype(jnp.bfloat16), "seq", scatter_dimension=1, tiled=True
        ).astype(jnp.float32),
        lax.psum_scatter(
            spreaded[10].astype(jnp.bfloat16), "seq", scatter_dimension=1, tiled=True
        ).astype(jnp.float32),
        lax.psum_scatter(
            spreaded[11].astype(jnp.bfloat16), "seq", scatter_dimension=1, tiled=True
        ).astype(jnp.float32),
        lax.psum_scatter(
            spreaded[12].astype(jnp.bfloat16), "seq", scatter_dimension=1, tiled=True
        ).astype(jnp.float32),
    )
    second_pass = (
        lax.psum_scatter(first_pass[0], "dp", scatter_dimension=0, tiled=True),
        lax.psum_scatter(first_pass[1], "dp", scatter_dimension=0, tiled=True),
        lax.psum_scatter(first_pass[2], "dp", scatter_dimension=0, tiled=True),
        lax.psum_scatter(first_pass[3], "dp", scatter_dimension=0, tiled=True),
        lax.psum_scatter(first_pass[4], "dp", scatter_dimension=0, tiled=True),
        lax.psum_scatter(first_pass[5], "dp", scatter_dimension=0, tiled=True),
        lax.psum_scatter(first_pass[6], "dp", scatter_dimension=0, tiled=True),
        lax.psum_scatter(first_pass[7], "dp", scatter_dimension=0, tiled=True),
        lax.psum_scatter(first_pass[8], "dp", scatter_dimension=0, tiled=True),
        lax.psum_scatter(first_pass[9], "dp", scatter_dimension=0, tiled=True),
        lax.psum_scatter(first_pass[10], "dp", scatter_dimension=0, tiled=True),
        lax.psum_scatter(first_pass[11], "dp", scatter_dimension=0, tiled=True),
        lax.psum_scatter(first_pass[12], "dp", scatter_dimension=0, tiled=True),
    )
    reduced = [unpack(member) for member in second_pass]
    return (
        layer_output,
        frames_grad,
        reduced[0],
        reduced[1],
        reduced[2],
        reduced[3],
        reduced[4],
        reduced[5],
        reduced[6],
        reduced[7],
        reduced[8],
        reduced[9],
        reduced[10],
        reduced[11],
        modulation_weight_grad,
        reduced[12],
    )


def hand_over_kernel(count, *refs):
    copies = [
        pltpu.make_async_copy(source, target, refs[-1].at[n])
        for n, (source, target) in enumerate(zip(refs[:count], refs[count : 2 * count]))
    ]
    for copy in copies:
        copy.start()
    for copy in copies:
        copy.wait()


def hand_over(*arrays):
    anywhere = pl.BlockSpec(memory_space=pl.ANY)
    return pl.pallas_call(
        partial(hand_over_kernel, len(arrays)),
        out_shape=[jax.ShapeDtypeStruct(array.shape, array.dtype) for array in arrays],
        in_specs=[pl.BlockSpec(memory_space=pltpu.VMEM)] * len(arrays),
        out_specs=[anywhere] * len(arrays),
        scratch_shapes=[pltpu.SemaphoreType.DMA((len(arrays),))],
    )(*arrays)


def on_device_fast(
    frames, output_gradient, segment_lengths, time_index, query_weight, query_bias, key_weight, key_bias,
    value_weight, value_bias, output_projection, output_bias, up_weight, up_bias, down_weight, down_bias,
    modulation_weight, modulation_bias,
):
    seq_index, dp_index = lax.axis_index("seq"), lax.axis_index("dp")
    depth = lax.axis_size("dp") // 2
    own_index = dp_index * 4 + seq_index
    _, span, width = frames.shape
    own_rows, hidden = up_weight.shape
    down_rows = down_weight.shape[0]
    vectors = (query_bias, key_bias, value_bias, output_bias, up_bias, down_bias, modulation_bias)
    biases = [vector.reshape(1, -1) for vector in vectors]
    (output, grad_middle, mg_in, bias_in, mods, low, gwo, gup, gdown, given_heads, qs, ks, vs, oh, lse, normed, wg,
     cosr, sinr) = forward_call(
        depth, span, own_rows, down_rows, hidden,
        (segment_lengths, time_index, frames[0], output_gradient[0], *biases, query_weight, key_weight, value_weight,
         output_projection, up_weight, down_weight, modulation_weight),
    )
    (fgrad, dwq, dwk, dwv, dwo, dup, ddown, dmw, mbias, btile) = backward_call(
        depth, span, own_rows, down_rows, hidden,
        (segment_lengths, given_heads, qs, ks, vs, oh, lse, normed, wg, cosr, sinr, low, mods, frames[0],
         grad_middle, mg_in, bias_in,
         gwo, gup, gdown),
    )
    sums = btile.reshape(-1)

    def own_part(vector, start, size):
        return lax.dynamic_slice_in_dim(vector, start + own_index * size, size)

    lengths = [member.shape[0] for member in (query_bias, key_bias, value_bias, output_bias, up_bias, down_bias)]
    starts = [sum(lengths[:n]) * depth * 8 for n in range(6)]
    bq, bk, bv, bo, bu, bd = [own_part(sums, start, size) for start, size in zip(starts, lengths)]
    bm = own_part(mbias[0], 0, modulation_bias.shape[0])
    output, fgrad, dwq, dwk, dwv, dwo, dup, ddown, dmw = hand_over(
        output, fgrad, dwq, dwk, dwv, dwo, dup, ddown, dmw
    )
    return (
        output[None], fgrad[None], dwq, bq, dwk, bk, dwv, bv, dwo, bo, dup, bu, ddown, bd, dmw, bm,
    )


def fits(mesh, frames, *parameters):
    dp, seq = mesh.shape["dp"], mesh.shape["seq"]
    rows = parameters[3].shape[0] // (dp * seq)
    return seq == 4 and dp % 2 == 0 and rows == 32 and frames.shape[0] == dp


def solution(mesh):
    def run(*arrays):
        return mapped(mesh, on_device_fast if fits(mesh, *arrays) else on_device)(*arrays)

    return run


def mapped(mesh, body):
    return jax.shard_map(
        body,
        mesh=mesh,
        in_specs=(
            P("dp", "seq", None),
            P("dp", "seq", None),
            P("dp", None),
            P("dp", None),
            P(("dp", "seq"), None),
            P(("dp", "seq")),
            P(("dp", "seq"), None),
            P(("dp", "seq")),
            P(("dp", "seq"), None),
            P(("dp", "seq")),
            P(("dp", "seq"), None),
            P(("dp", "seq")),
            P(("dp", "seq"), None),
            P(("dp", "seq")),
            P(("dp", "seq"), None),
            P(("dp", "seq")),
            P(("dp", "seq"), None),
            P(("dp", "seq")),
        ),
        out_specs=(
            P("dp", "seq", None),
            P("dp", "seq", None),
            P(("dp", "seq"), None),
            P(("dp", "seq")),
            P(("dp", "seq"), None),
            P(("dp", "seq")),
            P(("dp", "seq"), None),
            P(("dp", "seq")),
            P(("dp", "seq"), None),
            P(("dp", "seq")),
            P(("dp", "seq"), None),
            P(("dp", "seq")),
            P(("dp", "seq"), None),
            P(("dp", "seq")),
            P(("dp", "seq"), None),
            P(("dp", "seq")),
        ),
        check_vma=False,
    )
```

profile of v0, /device:TPU:0, one launch (start us, length us, event | category | flops | bytes accessed | tf_op | source)
XLA Modules:
  0.0 217.1 jit_solution(16235994271965789019)
XLA Ops:
  0.6 1.2 reshape.63.bm
  1.9 111.3 %shard_map.297 = (bf16[384,1024]{1,0:T(8,128)(2,1)}, f32[384,1024]{1,0:T(8,128)}, f32[16,1024]{1,0:T(8,128)}, f32[56,128]{1,0:T(8,128)}, f32[8,6144]{1,0:T(8,128...) custom-call(s32[1,4]{1,0:T(1,128)} %lens.3, ...), custom_call_target="tpu_custom_call" | custom-call | flops 20000000000 | bytes 60000000 | tf_op jit(solution)/shard_map/pallas_call | solution.py:839
  113.1 95.6 %shard_map.298 = (bf16[384,1024]{1,0:T(8,128)(2,1)}, f32[32,1024]{1,0:T(8,128)}, f32[32,1024]{1,0:T(8,128)}, f32[32,1024]{1,0:T(8,128)}, f32[32,1024]{1,0:T(8,12...) custom-call(s32[1,4]{1,0:T(1,128)} %lens.3, ...), custom_call_target="tpu_custom_call" | custom-call | flops 20000000000 | bytes 40000000 | tf_op jit(solution)/shard_map/pallas_call | solution.py:1382
  208.7 3.8 %shard_map.299 = (bf16[384,1024]{1,0:T(8,128)(2,1)}, bf16[384,1024]{1,0:T(8,128)(2,1)}, f32[32,1024]{1,0:T(8,128)}, f32[32,1024]{1,0:T(8,128)}, f32[32,1024]{1,0...) custom-call(bf16[384,1024]{1,0:T(8,128)(2,1)} %get-tuple-element.54.refs_0_, ...), custom_call_target="tpu_custom_call" | custom-call | tf_op jit(solution)/shard_map/pallas_call | solution.py:1891
  212.5 1.3 fusion
  213.8 1.3 dynamic_slice.27
  215.1 0.9 slice.3
  216.1 0.6 constant_dynamic-slice_fusion
where the time goes:
time: 220 us; the launch traced here: 217 us
  Pallas kernels  211 us (96%)
  local copies, waits for them, and re-layouts  5.37 us (2%)
    pallas_call x1, Pallas kernels, forward_call(): pl.pallas_call(partial(forward_kernel, depth), out_shape=[shape for shape...  111 us
    pallas_call x1, Pallas kernels, backward_call(): pl.pallas_call(partial(backward_kernel, depth), out_shape=[shape for shap...  95.6 us

commit v1 on v0

--- a/solution.py
+++ b/solution.py
@@ -135,6 +135,11 @@
 
 def product(left, right):
     return jnp.dot(left, right, preferred_element_type=F32)
+
+
+def straight(first, last, body):
+    for step in range(first, last):
+        body(step, 0)
 
 
 AXES = (
@@ -587,7 +592,7 @@
             branch[:, columns] = product(att[...], wo_columns(columns)) + rowbias[0:1, columns]
             return carry
 
-        lax.fori_loop(0, width // tile, body, 0)
+        straight(0, width // tile, body)
 
         def norm_forward(step, carry):
             rows = pl.ds(pl.multiple_of(step * block, block), block)
@@ -601,7 +606,7 @@
             normed_two[rows, :] = (hat * (1.0 + scale) + shift).astype(BF16)
             return carry
 
-        lax.fori_loop(0, span // block, norm_forward, 0)
+        straight(0, span // block, norm_forward)
 
     root = math.sqrt(2.0 / math.pi)
 
@@ -620,7 +625,7 @@
             )
             return carry
 
-        lax.fori_loop(side * width // tile, (side + 1) * width // tile, body, 0)
+        straight(side * width // tile, (side + 1) * width // tile, body)
 
     def go_down():
         arrived(6, 7, 8, 9)
@@ -636,7 +641,7 @@
             sums[:, shifted(3, step)] = by_segment(members(0, span), back * value)
             return carry
 
-        lax.fori_loop(0, width // tile, body, 0)
+        straight(0, width // tile, body)
 
     def back_values():
         def hidden_tile(step, carry):
@@ -645,13 +650,13 @@
             gh[:, rows] = (across(gbt[...], weight) * slope[:, rows]).astype(BF16)
             return carry
 
-        lax.fori_loop(0, hidden // tile, hidden_tile, 0)
+        straight(0, hidden // tile, hidden_tile)
 
         def normed_tile(step, carry):
             gn[:, tile_at(step)] = across(gh[...], up_all[step].reshape(tile, hidden))
             return carry
 
-        lax.fori_loop(0, width // tile, normed_tile, 0)
+        straight(0, width // tile, normed_tile)
         sums[:, : 3 * width] = jnp.zeros((16, 3 * width), F32)
 
         def norm_back(step, carry):
@@ -672,7 +677,7 @@
             sums[:, 2 * width : 3 * width] += by_segment(inside, grad * hat)
             return carry
 
-        lax.fori_loop(0, span // block, norm_back, 0)
+        straight(0, span // block, norm_back)
         sent["o"] = []
         mine = pl.ds(pl.multiple_of(g * span, span), span)
         for k in (1, 2, 3, 0):
@@ -696,7 +701,7 @@
             down_all[step // 2, step % 2] = grad.reshape(down_all.shape[2:])
             return carry
 
-        lax.fori_loop(0, hidden // tile, down_tile, 0)
+        straight(0, hidden // tile, down_tile)
         stores.append(move.local(down_all, gdown))
 
         def up_tile(step, carry):
@@ -704,7 +709,7 @@
             up_all[step] = grad.reshape(up_all.shape[1:])
             return carry
 
-        lax.fori_loop(0, width // tile, up_tile, 0)
+        straight(0, width // tile, up_tile)
         stores.append(move.local(up_all, gup))
 
         def out_tile(step, carry):
@@ -712,7 +717,7 @@
             wo_all[step] = grad.reshape(wo_all.shape[1:])
             return carry
 
-        lax.fori_loop(0, width // tile, out_tile, 0)
+        straight(0, width // tile, out_tile)
         stores.append(move.local(wo_all, gwo))
         ones = jnp.ones((16, span), BF16)
         btile[0:24, :] = jnp.zeros((24, LANES), F32)
@@ -1073,7 +1078,7 @@
             gnp[target, pl.ds(pl.multiple_of(step * block, block), block), :] = total.astype(BF16)
             return carry
 
-        lax.fori_loop(0, span // block, body, 0)
+        straight(0, span // block, body)
 
     away_other, away_same = (1 - x) * 2 + (1 - c), (1 - x) * 2 + c
     home_other = x * 2 + (1 - c)
@@ -1114,7 +1119,7 @@
                 gw[j, step // per, (step % per) * (tile // (4 * shard)) + n] = lead[n]
             return carry
 
-        lax.fori_loop(0, MODEL_WIDTH // tile, body, 0)
+        straight(0, MODEL_WIDTH // tile, body)
 
     gw_y, gw_z = {}, {}
 
@@ -1262,7 +1267,7 @@
     def norm_part():
         gn["home"].wait_recv()
         gn["x"].wait_recv()
-        lax.fori_loop(0, span // block, norm_rows, 0)
+        straight(0, span // block, norm_rows)
         late[0, 0:4, :] = acc_shift[0:4, :]
         late[0, 4:8, :] = acc_scale[0:4, :]
         mod_legs["row"] = [move.send(late.at[0], late.at[k], here.row_peer(k)) for k in (1, 2, 3)]

time: 220 us -> 212 us (0.964)
  Pallas kernels: 211 us -> 204 us
    pallas_call x1, Pallas kernels: 111 us -> 105 us  [forward_call(): pl.pallas_call(partial(forward_kernel, depth), out_shape=[shape for shape...]
where the time goes in v1:
time: 212 us; the launch traced here: 210 us
  Pallas kernels  204 us (96%)
  local copies, waits for them, and re-layouts  5.37 us (3%)
    pallas_call x1, Pallas kernels, forward_call(): pl.pallas_call(partial(forward_kernel, depth), out_shape=[shape for shape...  105 us
    pallas_call x1, Pallas kernels, backward_call(): pl.pallas_call(partial(backward_kernel, depth), out_shape=[shape for shap...  94.7 us

profile of v1, /device:TPU:0, one launch (start us, length us, event | category | flops | bytes accessed | tf_op | source)
XLA Modules:
  0.0 209.8 jit_solution(7113085905410140511)
XLA Ops:
  0.6 1.2 reshape.63.bm
  1.9 105.1 %shard_map.297 = (bf16[384,1024]{1,0:T(8,128)(2,1)}, f32[384,1024]{1,0:T(8,128)}, f32[16,1024]{1,0:T(8,128)}, f32[56,128]{1,0:T(8,128)}, f32[8,6144]{1,0:T(8,128...) custom-call(s32[1,4]{1,0:T(1,128)} %lens.3, ...), custom_call_target="tpu_custom_call" | custom-call | flops 20000000000 | bytes 60000000 | tf_op jit(solution)/shard_map/pallas_call | solution.py:844
  106.9 94.7 %shard_map.298 = (bf16[384,1024]{1,0:T(8,128)(2,1)}, f32[32,1024]{1,0:T(8,128)}, f32[32,1024]{1,0:T(8,128)}, f32[32,1024]{1,0:T(8,128)}, f32[32,1024]{1,0:T(8,12...) custom-call(s32[1,4]{1,0:T(1,128)} %lens.3, ...), custom_call_target="tpu_custom_call" | custom-call | flops 20000000000 | bytes 40000000 | tf_op jit(solution)/shard_map/pallas_call | solution.py:1387
  201.6 3.8 %shard_map.299 = (bf16[384,1024]{1,0:T(8,128)(2,1)}, bf16[384,1024]{1,0:T(8,128)(2,1)}, f32[32,1024]{1,0:T(8,128)}, f32[32,1024]{1,0:T(8,128)}, f32[32,1024]{1,0...) custom-call(bf16[384,1024]{1,0:T(8,128)(2,1)} %get-tuple-element.54.refs_0_, ...), custom_call_target="tpu_custom_call" | custom-call | tf_op jit(solution)/shard_map/pallas_call | solution.py:1896
  205.4 1.3 fusion
  206.7 1.3 dynamic_slice.27
  208.0 0.9 slice.3
  209.0 0.6 constant_dynamic-slice_fusion

commit v2 on v1

--- a/solution.py
+++ b/solution.py
@@ -862,25 +862,26 @@
     return lax.dot_general(left, right, (((0,), (0,)), ((), ())), preferred_element_type=F32)
 
 
-X_FIRST = (0, 1, 0, 0, 1, 0, 0, 1, 0, 1)
+X_FIRST = (0, 1, 0, 1, 1, 1, 0, 0, 0, 1)
 (
     SUM_ONE, SUM_TWO, SUM_THREE, SUM_LAST, WEIGHTS_Y, WEIGHTS_Z, WEIGHTS_LAST, ATTEND_BACK, ROWS_AWAY,
     ROWS_ACROSS, ROWS_HOME, NORM, EARLY_CORE, EARLY_X, EARLY_Z, EARLY_Y, EARLY_SHARE, EARLY_DONE, LATE_ROWS,
     LATE_DONE, BIAS_START, BIAS_NEXT, BIAS_DONE,
 ) = range(23)
 BACKWARD_ORDER = (
-    (SUM_ONE, 0), (SUM_ONE, 4), (SUM_ONE, 3), (SUM_ONE, 2), (SUM_ONE, 5), (EARLY_CORE, 0), (SUM_ONE, 1),
-    (SUM_ONE, 6), (SUM_TWO, 0), (ATTEND_BACK, 3), (SUM_TWO, 3), (ATTEND_BACK, 1), (EARLY_X, 0), (SUM_ONE, 9),
-    (ATTEND_BACK, 1), (SUM_TWO, 1), (ATTEND_BACK, 1), (SUM_TWO, 4), (SUM_THREE, 3), (SUM_THREE, 0),
-    (ATTEND_BACK, 1), (EARLY_Z, 0), (SUM_TWO, 2), (SUM_TWO, 5), (SUM_ONE, 8), (SUM_TWO, 6), (ATTEND_BACK, 1),
-    (SUM_ONE, 7), (SUM_THREE, 1), (ATTEND_BACK, 1), (SUM_TWO, 9), (EARLY_Y, 0), (SUM_THREE, 4), (SUM_THREE, 5),
-    (ATTEND_BACK, 2), (SUM_THREE, 2), (SUM_THREE, 6), (ATTEND_BACK, 1), (SUM_THREE, 9), (SUM_TWO, 8),
-    (SUM_TWO, 7), (ROWS_AWAY, 0), (WEIGHTS_Y, 0), (ROWS_ACROSS, 0), (SUM_THREE, 8), (SUM_THREE, 7),
-    (WEIGHTS_Y, 2), (WEIGHTS_Z, 0), (BIAS_START, 0), (SUM_LAST, 3), (WEIGHTS_Y, 1), (ROWS_HOME, 0),
-    (SUM_LAST, 5), (BIAS_NEXT, 0), (WEIGHTS_Z, 2), (WEIGHTS_Z, 1), (WEIGHTS_LAST, 0), (SUM_LAST, 8), (NORM, 0),
-    (SUM_LAST, 2), (SUM_LAST, 1), (LATE_ROWS, 0), (SUM_LAST, 4), (BIAS_NEXT, 0), (WEIGHTS_LAST, 1),
-    (BIAS_NEXT, 0), (EARLY_SHARE, 0), (WEIGHTS_LAST, 2), (LATE_DONE, 0), (SUM_LAST, 6), (SUM_LAST, 0),
-    (EARLY_DONE, 0), (SUM_LAST, 7), (SUM_LAST, 9), (BIAS_DONE, 0),
+    (SUM_ONE, 0), (ATTEND_BACK, 1), (SUM_ONE, 1), (SUM_ONE, 2), (ATTEND_BACK, 1), (SUM_ONE, 4),
+    (ATTEND_BACK, 1), (SUM_TWO, 0), (SUM_ONE, 6), (EARLY_CORE, 0), (ATTEND_BACK, 1), (SUM_ONE, 5),
+    (ATTEND_BACK, 1), (SUM_TWO, 1), (ATTEND_BACK, 1), (SUM_TWO, 6), (SUM_ONE, 7), (SUM_TWO, 4), (SUM_TWO, 2),
+    (ATTEND_BACK, 1), (SUM_THREE, 0), (SUM_THREE, 1), (ATTEND_BACK, 1), (SUM_TWO, 5), (EARLY_X, 0),
+    (SUM_ONE, 9), (SUM_ONE, 8), (SUM_THREE, 6), (SUM_TWO, 7), (ATTEND_BACK, 1), (EARLY_Z, 0), (ATTEND_BACK, 1),
+    (SUM_THREE, 5), (SUM_THREE, 2), (ATTEND_BACK, 1), (SUM_TWO, 9), (SUM_THREE, 4), (SUM_ONE, 3), (EARLY_Y, 0),
+    (ATTEND_BACK, 1), (SUM_THREE, 9), (WEIGHTS_Y, 1), (SUM_TWO, 8), (ROWS_AWAY, 0), (SUM_THREE, 7),
+    (SUM_LAST, 1), (SUM_LAST, 4), (SUM_LAST, 5), (SUM_TWO, 3), (ROWS_ACROSS, 0), (SUM_THREE, 8), (WEIGHTS_Y, 2),
+    (WEIGHTS_Z, 1), (SUM_LAST, 7), (WEIGHTS_Y, 0), (BIAS_START, 0), (SUM_LAST, 8), (SUM_LAST, 6),
+    (EARLY_SHARE, 0), (SUM_THREE, 3), (WEIGHTS_Z, 2), (ROWS_HOME, 0), (WEIGHTS_Z, 0), (BIAS_NEXT, 0),
+    (SUM_LAST, 9), (SUM_LAST, 0), (SUM_LAST, 3), (NORM, 0), (SUM_LAST, 2), (LATE_ROWS, 0), (WEIGHTS_LAST, 2),
+    (BIAS_NEXT, 0), (WEIGHTS_LAST, 0), (WEIGHTS_LAST, 1), (BIAS_NEXT, 0), (EARLY_DONE, 0), (LATE_DONE, 0),
+    (BIAS_DONE, 0),
 )
 
 
@@ -1000,8 +1001,6 @@
         return move.send(btile, brecv.at[slot], peer)
 
     block = 128
-    for copy in loads:
-        copy.wait()
 
     def columns_of_segments(step, carry):
         rows = pl.ds(pl.multiple_of(step * block, block), block)
@@ -1015,7 +1014,11 @@
             va[pair, rows, LANES:] = jnp.where(lane < 3, 1.0, 0.0).astype(BF16)
         return carry
 
+    for copy in loads[:2]:
+        copy.wait()
     lax.fori_loop(0, rows_all // block, columns_of_segments, 0)
+    for copy in loads[2:]:
+        copy.wait()
 
     tall = 256
     steps = rows_all // tall
@@ -1084,9 +1087,12 @@
     home_other = x * 2 + (1 - c)
     gn = {}
 
+    def need_late():
+        while late_loads:
+            late_loads.pop().wait()
+
     def rows_away():
-        for copy in late_loads:
-            copy.wait()
+        need_late()
         back_rows(away_other)
         gn["core"] = move.send(gnp.at[away_other], gnr.at[0], here.core())
 
@@ -1124,6 +1130,7 @@
     gw_y, gw_z = {}, {}
 
     def weights_y(j):
+        need_late()
         weight_rows(j)
         gw_y[j] = move.send(gw.at[j, :, 1 - y], gwy.at[j], here.across_y())
 
@@ -1880,26 +1887,41 @@
     )
 
 
-def hand_over_kernel(count, *refs):
+def hand_over_kernel(count, lengths, *refs):
+    sources, refs = refs[: count + 2], refs[count + 2 :]
+    targets, vectors, sems = refs[:count], refs[count:-1], refs[-1]
     copies = [
-        pltpu.make_async_copy(source, target, refs[-1].at[n])
-        for n, (source, target) in enumerate(zip(refs[:count], refs[count : 2 * count]))
+        pltpu.make_async_copy(sources[n], targets[n], sems.at[n]) for n in range(count)
     ]
     for copy in copies:
         copy.start()
+    index = lax.axis_index("dp") * 4 + lax.axis_index("seq")
+    sums, strip = sources[count], sources[count + 1]
+    first = 0
+    for vector, size in zip(vectors, lengths):
+        start = index * size
+        row = sums[pl.ds(first + start // LANES, 1), :]
+        vector[...] = pltpu.roll(row, (LANES - start % LANES) % LANES, 1)[:, :size]
+        first += size * lax.axis_size("dp") * 4 // LANES
+    size = vectors[-1].shape[1]
+    start = index * size
+    wide = strip[0:1, pl.ds(pl.multiple_of(start // LANES * LANES, LANES), 2 * LANES)]
+    vectors[-1][...] = pltpu.roll(wide, (2 * LANES - start % LANES) % (2 * LANES), 1)[:, :size]
     for copy in copies:
         copy.wait()
 
 
-def hand_over(*arrays):
-    anywhere = pl.BlockSpec(memory_space=pl.ANY)
+def hand_over(lengths, arrays, sums, strip):
+    anywhere, vmem = pl.BlockSpec(memory_space=pl.ANY), pl.BlockSpec(memory_space=pltpu.VMEM)
+    count = len(arrays)
     return pl.pallas_call(
-        partial(hand_over_kernel, len(arrays)),
-        out_shape=[jax.ShapeDtypeStruct(array.shape, array.dtype) for array in arrays],
-        in_specs=[pl.BlockSpec(memory_space=pltpu.VMEM)] * len(arrays),
-        out_specs=[anywhere] * len(arrays),
-        scratch_shapes=[pltpu.SemaphoreType.DMA((len(arrays),))],
-    )(*arrays)
+        partial(hand_over_kernel, count, lengths[:-1]),
+        out_shape=[jax.ShapeDtypeStruct(array.shape, array.dtype) for array in arrays]
+        + [jax.ShapeDtypeStruct((1, size), F32) for size in lengths],
+        in_specs=[vmem] * (count + 2),
+        out_specs=[anywhere] * count + [vmem] * len(lengths),
+        scratch_shapes=[pltpu.SemaphoreType.DMA((count,))],
+    )(*arrays, sums, strip)
 
 
 def on_device_fast(
@@ -1907,9 +1929,7 @@
     value_weight, value_bias, output_projection, output_bias, up_weight, up_bias, down_weight, down_bias,
     modulation_weight, modulation_bias,
 ):
-    seq_index, dp_index = lax.axis_index("seq"), lax.axis_index("dp")
     depth = lax.axis_size("dp") // 2
-    own_index = dp_index * 4 + seq_index
     _, span, width = frames.shape
     own_rows, hidden = up_weight.shape
     down_rows = down_weight.shape[0]
@@ -1927,18 +1947,11 @@
          grad_middle, mg_in, bias_in,
          gwo, gup, gdown),
     )
-    sums = btile.reshape(-1)
-
-    def own_part(vector, start, size):
-        return lax.dynamic_slice_in_dim(vector, start + own_index * size, size)
-
-    lengths = [member.shape[0] for member in (query_bias, key_bias, value_bias, output_bias, up_bias, down_bias)]
-    starts = [sum(lengths[:n]) * depth * 8 for n in range(6)]
-    bq, bk, bv, bo, bu, bd = [own_part(sums, start, size) for start, size in zip(starts, lengths)]
-    bm = own_part(mbias[0], 0, modulation_bias.shape[0])
-    output, fgrad, dwq, dwk, dwv, dwo, dup, ddown, dmw = hand_over(
-        output, fgrad, dwq, dwk, dwv, dwo, dup, ddown, dmw
-    )
+    lengths = tuple(vector.shape[0] for vector in vectors)
+    output, fgrad, dwq, dwk, dwv, dwo, dup, ddown, dmw, *parts = hand_over(
+        lengths, (output, fgrad, dwq, dwk, dwv, dwo, dup, ddown, dmw), btile, mbias
+    )
+    bq, bk, bv, bo, bu, bd, bm = [part.reshape(-1) for part in parts]
     return (
         output[None], fgrad[None], dwq, bq, dwk, bk, dwv, bv, dwo, bo, dup, bu, ddown, bd, dmw, bm,
     )

time: 212 us -> 206 us (0.972)
  local copies, waits for them, and re-layouts: 5.37 us -> 1.22 us
    dynamic_slice x3 -> x0, local copies, waits for them, and re-layouts: 3.21 us -> none  [own_part(): return lax.dynamic_slice_in_dim(vector, start + own_index * size, size)]
    pallas_call x1, Pallas kernels: 94.7 us -> 92.1 us  [backward_call(): pl.pallas_call(partial(backward_kernel, depth), out_shape=[shape for shap...]
where the time goes in v2:
time: 206 us; the launch traced here: 204 us
  Pallas kernels  202 us (98%)
    pallas_call x1, Pallas kernels, forward_call(): pl.pallas_call(partial(forward_kernel, depth), out_shape=[shape for shape...  105 us
    pallas_call x1, Pallas kernels, backward_call(): pl.pallas_call(partial(backward_kernel, depth), out_shape=[shape for shap...  92.1 us
    pallas_call x1, Pallas kernels, hand_over(): pl.pallas_call(partial(hand_over_kernel, count, lengths[:-1]), out_shape=...  4.4 us

profile of v2, /device:TPU:0, one launch (start us, length us, event | category | flops | bytes accessed | tf_op | source)
XLA Modules:
  0.0 203.9 jit_solution(12226979274440309891)
XLA Ops:
  0.6 1.2 reshape.80.bm
  1.9 105.0 %shard_map.297 = (bf16[384,1024]{1,0:T(8,128)(2,1)}, f32[384,1024]{1,0:T(8,128)}, f32[16,1024]{1,0:T(8,128)}, f32[56,128]{1,0:T(8,128)}, f32[8,6144]{1,0:T(8,128...) custom-call(s32[1,4]{1,0:T(1,128)} %lens.3, ...), custom_call_target="tpu_custom_call" | custom-call | flops 20000000000 | bytes 60000000 | tf_op jit(solution)/shard_map/pallas_call | solution.py:844
  106.9 92.1 %shard_map.298 = (bf16[384,1024]{1,0:T(8,128)(2,1)}, f32[32,1024]{1,0:T(8,128)}, f32[32,1024]{1,0:T(8,128)}, f32[32,1024]{1,0:T(8,128)}, f32[32,1024]{1,0:T(8,12...) custom-call(s32[1,4]{1,0:T(1,128)} %lens.3, ...), custom_call_target="tpu_custom_call" | custom-call | flops 20000000000 | bytes 40000000 | tf_op jit(solution)/shard_map/pallas_call | solution.py:1394
  199.1 4.4 %shard_map.299 = (bf16[384,1024]{1,0:T(8,128)(2,1)}, bf16[384,1024]{1,0:T(8,128)(2,1)}, f32[32,1024]{1,0:T(8,128)}, f32[32,1024]{1,0:T(8,128)}, f32[32,1024]{1,0...) custom-call(bf16[384,1024]{1,0:T(8,128)(2,1)} %get-tuple-element.61., ...), custom_call_target="tpu_custom_call" | custom-call | tf_op jit(solution)/shard_map/pallas_call | solution.py:1917

commit v3 on v2

--- a/solution.py
+++ b/solution.py
@@ -169,11 +169,11 @@
 def forward_kernel(
     depth,
     lens, times, frames, given_in, bq, bk, bv, bo, bu, bd, bm, wq, wk, wv, wo, up, down, mw,
-    output, gmid, mg, btile, mods, low, gwo, gup, gdown, do_all, qs_out, ks_out, vs_out, oh_out, lse_out,
+    output_out, gmid_out, mg, btile, mods, low, gwo, gup, gdown, do_all, qs_out, ks_out, vs_out, oh_out, lse_out,
     normed_out, wg_out, cos_out, sin_out,
     att, oh, qs, lse, normed, wg, cosr, sinr, rowbias, wo_all, up_all, down_all,
     bb, xall, mwst, tb, part, recva, suma, recvb, sumb, recvc, sumc, recvd, modh, bmat, mod3, qbias,
-    ka, va, qaug, given, mod6, branch, middle, normed_two, active, slope, gbt, gh, gn, gb, ga, sums,
+    output, gmid, ka, va, qaug, given, mod6, branch, middle, normed_two, active, slope, gbt, gh, gn, gb, ga, sums,
     send_sems, recv_sems, local_sems,
 ):
     here = Place(depth)
@@ -642,6 +642,7 @@
             return carry
 
         straight(0, width // tile, body)
+        stores.append(move.local(output, output_out))
 
     def back_values():
         def hidden_tile(step, carry):
@@ -678,6 +679,7 @@
             return carry
 
         straight(0, span // block, norm_back)
+        stores.append(move.local(gmid, gmid_out))
         sent["o"] = []
         mine = pl.ds(pl.multiple_of(g * span, span), span)
         for k in (1, 2, 3, 0):
@@ -771,8 +773,8 @@
     up_shape = (depth, 2, 2, 2, own_rows, hidden)
     down_shape = (depth, 2, 2, 2, down_rows, width)
     outs = [
-        (out((span, width), BF16), vmem),
-        (out((span, width), F32), vmem),
+        (out((span, width), BF16), anywhere),
+        (out((span, width), F32), anywhere),
         (out((16, width), F32), vmem),
         (out((56, LANES), F32), vmem),
         (out((8, 6 * width), F32), vmem),
@@ -821,6 +823,8 @@
         pltpu.VMEM((64 * depth, LANES), BF16),
         pltpu.VMEM((16, 2 * width), F32),
         pltpu.VMEM((8, own_width), F32),
+        low,
+        wide,
         pltpu.VMEM((2, rows_all, 2 * LANES), BF16),
         pltpu.VMEM((2, rows_all, 2 * LANES), BF16),
         pltpu.VMEM(table, BF16),
@@ -887,11 +891,12 @@
 
 def backward_kernel(
     depth,
-    lens, do_in, qs_in, ks_in, vs_in, oh_in, lse_in, normed_in, wg_in, cos_in, sin_in, low, mods, frames, gmid,
+    lens, do_in, qs_in, ks_in, vs_in, oh_in, lse_in, normed_in, wg_in, cos_in, sin_in, low, mods, frames_in, gmid_in,
     mg_in, bias_in, gwo, gup, gdown,
     fgrad, dwq, dwk, dwv, dwo, dup, ddown, dmw, mbias, btile,
     qs, do, oh, lse, normed, wg, cosr, sinr, ka, va, qaug, dk_sum, dv_sum, gr, gw, gwy, gwz, gsum,
     gnp, gnr, gnx, mod3, acc_shift, acc_scale, mg, mgr, mgs, mgx, ev, late, joined, ez, brecv, bz,
+    frames, gmid,
     *rest,
 ):
     send_sems, recv_sems, local_sems = rest[-3:]
@@ -946,6 +951,7 @@
         legs[f] = move.send(source.at[:, :, :, 1 - c], first[f], here.core())
         held.append(move.local(source.at[:, :, :, c], own[f]))
     late_loads = [move.local(normed_in, normed), move.local(wg_in, wg)]
+    late_loads += [move.local(frames_in, frames), move.local(gmid_in, gmid)]
 
     def sum_first(f):
         legs[f].wait_recv()
@@ -1386,6 +1392,8 @@
         pltpu.VMEM((depth, 2, 16, half), BF16),
         pltpu.VMEM((3, 56, LANES), F32),
         pltpu.VMEM((depth - 1, 56, LANES), F32),
+        pltpu.VMEM((span, MODEL_WIDTH), BF16),
+        pltpu.VMEM((span, MODEL_WIDTH), F32),
     ]
     piece = (own_rows // 2, MODEL_WIDTH)
     for lead in ((depth, 2, 2), (depth, 2, 2), (depth, 2), (depth,), (depth - 1,)):
@@ -1394,7 +1402,7 @@
     return pl.pallas_call(
         partial(backward_kernel, depth),
         out_shape=[shape for shape, _ in outs],
-        in_specs=[scalar] + [anywhere] * 10 + [vmem] * 6 + [anywhere] * 3,
+        in_specs=[scalar] + [anywhere] * 10 + [vmem] * 2 + [anywhere] * 2 + [vmem] * 2 + [anywhere] * 3,
         out_specs=[spec for _, spec in outs],
         scratch_shapes=scratch,
         compiler_params=pltpu.CompilerParams(

time: 206 us -> 205 us (level)
  no operation moved by 1% of the time
where the time goes in v3:
time: 205 us; the launch traced here: 202 us
  Pallas kernels  200 us (98%)
    pallas_call x1, Pallas kernels, forward_call(): pl.pallas_call(partial(forward_kernel, depth), out_shape=[shape for shape...  104 us
    pallas_call x1, Pallas kernels, backward_call(): pl.pallas_call(partial(backward_kernel, depth), out_shape=[shape for shap...  91.4 us
    pallas_call x1, Pallas kernels, hand_over(): pl.pallas_call(partial(hand_over_kernel, count, lengths[:-1]), out_shape=...  4.4 us

profile of v3, /device:TPU:0, one launch (start us, length us, event | category | flops | bytes accessed | tf_op | source)
XLA Modules:
  0.0 202.4 jit_solution(2782629051717545999)
XLA Ops:
  0.6 1.2 reshape.80.bm
  1.9 104.3 %shard_map.297 = (bf16[384,1024]{1,0:T(8,128)(2,1)}, f32[384,1024]{1,0:T(8,128)}, f32[16,1024]{1,0:T(8,128)}, f32[56,128]{1,0:T(8,128)}, f32[8,6144]{1,0:T(8,128...) custom-call(s32[1,4]{1,0:T(1,128)} %lens.3, ...), custom_call_target="tpu_custom_call" | custom-call | flops 20000000000 | bytes 60000000 | tf_op jit(solution)/shard_map/pallas_call | solution.py:848
  106.2 91.4 %shard_map.298 = (bf16[384,1024]{1,0:T(8,128)(2,1)}, f32[32,1024]{1,0:T(8,128)}, f32[32,1024]{1,0:T(8,128)}, f32[32,1024]{1,0:T(8,128)}, f32[32,1024]{1,0:T(8,12...) custom-call(s32[1,4]{1,0:T(1,128)} %lens.3, ...), custom_call_target="tpu_custom_call" | custom-call | flops 20000000000 | bytes 40000000 | tf_op jit(solution)/shard_map/pallas_call | solution.py:1402
  197.6 4.4 %shard_map.299 = (bf16[384,1024]{1,0:T(8,128)(2,1)}, bf16[384,1024]{1,0:T(8,128)(2,1)}, f32[32,1024]{1,0:T(8,128)}, f32[32,1024]{1,0:T(8,128)}, f32[32,1024]{1,0...) custom-call(bf16[384,1024]{1,0:T(8,128)(2,1)} %get-tuple-element.61., ...), custom_call_target="tpu_custom_call" | custom-call | tf_op jit(solution)/shard_map/pallas_call | solution.py:1925
